TPU v7x, 128 devices: a whole 4x4x4 slice. The times are simulated.
128 devices in a mesh: freq: 8 (over x, core), slab: 16 (over y, z).
Axes of the slice: x: 4, y: 4, z: 4, core: 2. Of those that a mesh axis runs over, the one named last changes fastest.
Arguments:
- traces: bfloat16 [393216, 2048], P(('freq', 'slab')), may hold values from -6 to 6
- trace_counts: int32 [128, 8], P(('freq', 'slab')), may hold values from 1 to 512, 3072 in all within a row
- aperture_start: int32 [1024], P(('freq', 'slab')), may hold values from 0 to 511
- shot_position: int32 [1024], P(('freq', 'slab')), may hold values from 0 to 4095
- rec_slot: int32 [512], replicated, may hold values from 0 to 767, as said below
Outputs:
- encoded: bfloat16 [768, 256, 256], P('slab', 'freq')
Inputs may be any that keep to these rules, and one draw needn't show every extreme that they name: `rec_slot`: distinct receivers have distinct slots. No depth slab owns more than 48 receivers, at least one owns exactly 48, and slots 0 and 767 are always used.
All inputs are finite; a program needn't handle non-finite values.
Results may differ from a plain program's by a relative error of at most 0.0062.
Values may be sent and summed in bfloat16 or wider, within the bound.
No kernel may reach another device: no remote copies, remote signals or barrier semaphores. Data moves between devices by JAX's collectives and lax.ppermute only.
A program may use at most 192 MiB of HBM per device.

v0:
```python
import math

import jax
import jax.numpy as jnp
from jax import lax
from jax.sharding import PartitionSpec as P

NT = 2048
FREQUENCY_COUNT = 256
F0 = 8
RAY_PARAM_COUNT = 128
NREC = 512
RDIV = 16


def dft_factors(freq_bins, samples):
    sample_index = jnp.arange(samples, dtype=jnp.int32)
    phase_index = jnp.remainder(sample_index[:, None] * freq_bins[None, :], samples)
    angle_rad = phase_index.astype(jnp.float32) * (2.0 * math.pi / samples)
    factor = 1.0 / math.sqrt(samples)
    return (
        (jnp.cos(angle_rad) * factor).astype(jnp.bfloat16),
        (-jnp.sin(angle_rad) * factor).astype(jnp.bfloat16),
    )


def phase_blocks(freq_bins, positions, total_shots):
    ray_offset = jnp.arange(RAY_PARAM_COUNT, dtype=jnp.int32) - RAY_PARAM_COUNT // 2
    period = NT * RDIV
    product = (
        freq_bins[:, None, None, None]
        * ray_offset[None, None, None, :]
        * positions[None, :, :, None]
    )
    angle_rad = jnp.remainder(product, period).astype(jnp.float32) * (2.0 * math.pi / period)
    factor = 1.0 / math.sqrt(total_shots)
    cosine = (jnp.cos(angle_rad) * factor).astype(jnp.bfloat16)
    sine_part = (jnp.sin(angle_rad) * factor).astype(jnp.bfloat16)
    upper_half = jnp.concatenate([cosine, -sine_part], axis=3)
    lower_half = jnp.concatenate([sine_part, cosine], axis=3)
    stacked = jnp.stack([upper_half, lower_half], axis=2)
    return stacked.reshape(
        freq_bins.shape[0], positions.shape[0] * 2 * positions.shape[1], 2 * RAY_PARAM_COUNT
    )


def frequency_spectra(transform, traces):
    return lax.dot_general(
        transform, traces, (((0,), (1,)), ((), ())), preferred_element_type=jnp.float32
    ).astype(jnp.bfloat16)


def receiver_index(counts, starts, row_total, shot_total):
    shot_count = counts.shape[0]
    by_source = counts.reshape(shot_count // shot_total, shot_total)
    inclusive = jnp.cumsum(by_source, axis=1)
    source_base = (jnp.arange(shot_count // shot_total, dtype=jnp.int32) * row_total)[:, None]
    begins = (source_base + inclusive - by_source).reshape(shot_count)
    receivers = jnp.arange(NREC, dtype=jnp.int32)
    offset = jnp.remainder(receivers[None, :] - starts[:, None], NREC)
    valid = offset < counts[:, None]
    picks = jnp.where(valid, begins[:, None] + offset, 0)
    return (picks, valid)


def slot_matrix(rec_slot, slot_count):
    return (rec_slot[:, None] == jnp.arange(slot_count, dtype=jnp.int32)[None, :]).astype(
        jnp.bfloat16
    )


def slot_grid(
    owned_spectra, counts, starts, row_total, shot_total, slot_count, freq_block, rec_slot
):
    picks, valid = receiver_index(counts, starts, row_total, shot_total)
    shot_count = counts.shape[0]
    picked = jnp.take(owned_spectra, picks.reshape(-1), axis=1)
    picked = picked.reshape(2, freq_block, shot_count, NREC)
    picked = jnp.where(valid[None, None, :, :], picked, jnp.zeros((), jnp.bfloat16))
    lattice = jnp.einsum(
        "rs,cfhr->sfch",
        slot_matrix(rec_slot, slot_count),
        picked,
        preferred_element_type=jnp.float32,
    )
    return lattice.astype(jnp.bfloat16).reshape(slot_count, freq_block, 2 * shot_count)


def on_device(traces, trace_counts, aperture_start, shot_position, rec_slot):
    row_total, samples = traces.shape
    shot_total = trace_counts.shape[1]
    freq_groups = lax.axis_size("freq")
    slab_groups = lax.axis_size("slab")
    freq_block = FREQUENCY_COUNT // freq_groups
    slot_cap = 3 * NREC // (2 * slab_groups)
    slot_count = slot_cap * slab_groups
    all_shots = shot_total * freq_groups * slab_groups
    column = jnp.arange(2 * FREQUENCY_COUNT, dtype=jnp.int32)
    owner_block = column // (2 * freq_block)
    within = column % (2 * freq_block)
    column_bins = F0 + owner_block * freq_block + within % freq_block
    cosine_table, sine_table = dft_factors(column_bins, samples)
    transform = jnp.where((within // freq_block == 0)[None, :], cosine_table, sine_table)
    local_bins = F0 + lax.axis_index("freq") * freq_block + jnp.arange(freq_block, dtype=jnp.int32)
    own_counts = trace_counts[0]
    spectra = frequency_spectra(transform, traces)
    holder_counts, holder_starts, holder_positions = (
        lax.all_gather(own_counts, "freq", axis=0, tiled=True),
        lax.all_gather(aperture_start, "freq", axis=0, tiled=True),
        lax.all_gather(shot_position, "freq", axis=0, tiled=True),
    )
    owned_spectra = lax.all_to_all(spectra, "freq", split_axis=0, concat_axis=1, tiled=True)
    filled_lattice = slot_grid(
        owned_spectra,
        holder_counts,
        holder_starts,
        row_total,
        shot_total,
        slot_count,
        freq_block,
        rec_slot,
    )
    phases = phase_blocks(local_bins, holder_positions[None, :], all_shots)
    summed = lax.psum_scatter(
        jnp.einsum("xfs,fsq->xfq", filled_lattice, phases, preferred_element_type=jnp.float32),
        "slab",
        scatter_dimension=0,
        tiled=True,
    )
    return summed.astype(jnp.bfloat16)


def solution(mesh):
    return jax.shard_map(
        on_device,
        mesh=mesh,
        in_specs=(
            P(("freq", "slab"), None),
            P(("freq", "slab"), None),
            P(("freq", "slab")),
            P(("freq", "slab")),
            P(),
        ),
        out_specs=P("slab", "freq", None),
        check_vma=False,
    )
```

profile of v0, /device:TPU:1, one launch (start us, length us, event | category | flops | bytes accessed | tf_op | source)
XLA Modules:
  0.0 433.5 jit_solution(2946370972484755948)
XLA Ops:
  6.6 28.7 %convolution_convert_fusion = bf16[512,3072]{1,0:T(8,128)(2,1)} fusion(bf16[3072,2048]{1,0:T(8,128)(2,1)} %param.5, s32[512]{0:T(512)S(1)} %fusion.42, pred[512]{0:T(512)(128)(4,1)S(1)} %fusion.38), kind=kOutput, calls=%fused_computation.6 | convolution fusion | flops 6464995328 | bytes 15731200 | tf_op jit(solution)/shard_map/dot_general | solution.py:48
  35.3 0.0 copy-start.4
  35.3 0.0 copy-start.1
  35.3 0.0 copy-start.2
  35.3 0.0 copy-start.3
  35.3 6.1 %all-to-all-start = ((bf16[8,64,3072]{2,1,0:T(8,128)(2,1)}), bf16[8,64,3072]{2,1,0:T(8,128)(2,1)}, u32[]{:S(2)}, u32[]{:S(2)}) async-start(bf16[8,64,3072]{2,1,0:T(8,128)(2,1)} %bitcast.5), calls=%async_computation | async-start | bytes 6291456 | tf_op jit(solution)/shard_map/all_to_all | solution.py:112
  41.4 0.0 reduce-scatter.2.cloned.1.call-start
  41.4 0.0 copy-done.4
  41.4 0.6 dynamic-slice
  42.7 0.0 copy-done.1
  42.7 0.1 bitcast_dynamic-update-slice_fusion
  42.8 0.0 copy-done.2
  42.8 0.2 dynamic-update-slice
  43.0 0.0 copy-done.3
  43.0 0.2 dynamic-update-slice.1
  43.3 37.4 %all-reduce.3 = (s32[64]{0:T(128)S(1)}, s32[64]{0:T(128)S(1)}, s32[64]{0:T(128)S(1)}) all-reduce(s32[64]{0:T(128)S(1)} %dynamic-update-slice, s32[64]{0:T(128)S(1)} %bitcast_dynamic-update-slice_fusion, s32[64]{0:T(128)S(1)} %dynamic-update-slice.1), channel_id=1, replica_groups=mesh['freq'=8,'slab'=16] {'freq'}, use_global_device_ids=true, to_apply=%add | all-reduce | flops 192 | bytes 1536
  80.7 0.1 reshape.351
  80.8 0.2 reduce_window_sum.11
  81.0 0.1 broadcast_add_fusion
  81.0 0.1 add.184
  81.1 0.1 broadcast_bitcast_fusion.1
  81.2 0.1 copy.29
  81.3 0.1 fusion.33
  81.4 0.1 copy.27
  81.6 0.1 copy.28
  81.7 0.6 compare_select_fusion
  82.3 0.1 broadcast_multiply_fusion
  82.4 4.2 fusion.37
  86.6 4.6 %multiply_convert_fusion.3 = (bf16[32,1,64,128]{3,2,0,1:T(8,128)(2,1)S(1)}, bf16[32,1,64,128]{3,2,0,1:T(8,128)(2,1)S(1)}) fusion(s32[64]{0:T(128)S(1)} %get-tuple-element.5, s32[32,128]{1,0:T(8,128)S(1)} %broadcast_multiply_fusion), kind=kLoop, calls=%fused_computation.43 | loop fusion | flops 4718592 | bytes 1065216 | tf_op jit(solution)/shard_map/convert_element_type | solution.py:38
  91.2 0.3 maximum_bitcast_fusion
  91.6 0.2 pad_maximum_fusion
  91.8 0.1 copy.17
  91.9 0.2 broadcast_compare_fusion
  92.1 0.0 all-to-all-done
  92.1 6.6 %copy.18 = bf16[64,8,3072]{0,2,1:T(8,128)(2,1)} copy(bf16[64,8,3072]{2,0,1:T(8,128)(2,1)} %bitcast.6) | data formatting | bytes 6291456 | tf_op jit(solution)/shard_map/all_to_all | solution.py:112
  98.7 113.8 %gather_fusion = bf16[32768,64]{1,0:T(8,128)(2,1)} fusion(bf16[64,24576]{0,1:T(8,128)(2,1)} %bitcast.53, s32[32768]{0:T(1024)S(1)} %broadcast_clamp_fusion), kind=kCustom, calls=%fused_computation | custom fusion | bytes 8519680 | tf_op jit(solution)/shard_map/jit(_take)/gather | solution.py:77
  212.5 8.6 %copy.19 = bf16[64,32768]{1,0:T(8,128)(2,1)} copy(bf16[64,32768]{0,1:T(8,128)(2,1)} %bitcast.55) | data formatting | bytes 8388608 | tf_op jit(solution)/shard_map/jit(_take)/gather | solution.py:77
  221.1 0.0 copy-start
  221.1 3.8 copy.30
  224.9 0.0 copy-done
  224.9 5.8 %convert_bitcast_fusion = bf16[768,32,2,64]{0,3,1,2:T(8,128)(2,1)} fusion(pred[64,512]{1,0:T(8,128)(4,1)S(1)} %get-tuple-element.13, pred[64,512]{1,0:T(8,128)(4,1)S(1)} %get-tuple-element.12, s32[512]{0:T(512)S(1)} %copy-done, bf16[2,32,64,512]{3,2,1,0:T(8,128)(2,1)S(1)} %bitcast.58), kind=kOutput, calls=%fused_computation.2 | convolution fusion | flops 3228958720 | bytes 10553344 | tf_op jit(solution)/shard_map/rs,cfhr->sfch/dot_general | solution.py:80
  230.7 3.2 copy.20
  233.9 10.1 %convolution_bitcast_fusion = f32[768,32,256]{0,2,1:T(8,128)} fusion(bf16[32,128,256]{2,1,0:T(8,128)(2,1)S(1)} %bitcast.57, bf16[768,32,128]{0,2,1:T(8,128)(2,1)S(1)} %bitcast.54), kind=kOutput, calls=%fused_computation.1 | convolution fusion | flops 1610612736 | bytes 33554432 | tf_op jit(solution)/shard_map/xfs,fsq->xfq/dot_general | solution.py:125
  244.0 25.1 %copy.23 = f32[768,32,256]{2,1,0:T(8,128)} copy(f32[768,32,256]{0,2,1:T(8,128)} %convolution_bitcast_fusion) | data formatting | bytes 50331648 | tf_op jit(solution)/shard_map/xfs,fsq->xfq/transpose | solution.py:125
  269.1 0.0 reduce-scatter.2.cloned.1.call-update
  269.1 155.1 %reduce-scatter.2.cloned.1.call-done = f32[48,32,256]{2,1,0:T(8,128)} async-done(((f32[768,32,256]{2,1,0:T(8,128)}), f32[48,32,256]{2,1,0:T(8,128)}) %reduce-scatter.2.cloned.1.call-update) | async-done | bytes 1572880 | tf_op jit(solution)/shard_map/reduce_scatter | solution.py:124
  424.2 2.4 convert_element_type.76
  (10 shorter events, 0.1 us)
Async XLA Ops:
  35.3 6.2 %copy-start.4 = (u32[128]{0:T(128)S(1)}, u32[128]{0:T(128)}, u32[]{:S(2)}) copy-start(u32[128]{0:T(128)} %constant.147) | copy-start | bytes 1540
  35.3 7.4 %copy-start.1 = (s32[1,8]{1,0:T(1,128)S(1)}, s32[1,8]{1,0:T(1,128)}, u32[]{:S(2)}) copy-start(s32[1,8]{1,0:T(1,128)} %param.6) | copy-start | bytes 100
  35.3 7.5 %copy-start.2 = (s32[8]{0:T(128)S(1)}, s32[8]{0:T(128)}, u32[]{:S(2)}) copy-start(s32[8]{0:T(128)} %param.8) | copy-start | bytes 100
  35.3 7.8 %copy-start.3 = (s32[8]{0:T(128)S(1)}, s32[8]{0:T(128)}, u32[]{:S(2)}) copy-start(s32[8]{0:T(128)} %param.7) | copy-start | bytes 100
  35.3 56.8 %all-to-all-start = ((bf16[8,64,3072]{2,1,0:T(8,128)(2,1)}), bf16[8,64,3072]{2,1,0:T(8,128)(2,1)}, u32[]{:S(2)}, u32[]{:S(2)}) async-start(bf16[8,64,3072]{2,1,0:T(8,128)(2,1)} %bitcast.5), calls=%async_computation | async-start | bytes 6291456 | tf_op jit(solution)/shard_map/all_to_all | solution.py:112
  41.4 382.8 %reduce-scatter.2.cloned.1.call-start = ((), (), s32[]{:S(2)}) async-start(), calls=%async_computation.2 | async-start | bytes 26738688 | tf_op jit(solution)/shard_map/reduce_scatter | solution.py:124
  221.1 3.8 copy-start
Sparse Core Ops, SparseCore 0:
  269.2 154.9 reduce-scatter.1
where the time goes:
time: 434 us; the launch traced here: 433 us
  local copies, waits for them, and re-layouts  163 us (38%)
  waiting for transfers between devices  155 us (36%)
  matrix products  44.6 us (10%)
  blocking collectives  37.4 us (9%)
  between operations  14.2 us (3%)
  other arithmetic  12.9 us (3%)
  starting transfers between devices  6.13 us (1%)
    reduce_scatter x1, waiting for transfers between devices, on_device(): lax.psum_scatter(jnp.einsum('xfs,fsq->xfq', filled_lattice, phases, prefe...  155 us
    gather x2, local copies, waits for them, and re-layouts, slot_grid(): picked = jnp.take(owned_spectra, picks.reshape(-1), axis=1)  122 us
    unnamed x1, blocking collectives  37.4 us
    dot_general x1, matrix products, frequency_spectra(): lax.dot_general(transform, traces, (((0,), (1,)), ((), ())), preferred_el...  28.7 us
    transpose x1, local copies, waits for them, and re-layouts, on_device(): jnp.einsum('xfs,fsq->xfq', filled_lattice, phases, preferred_element_type...  25.1 us
    dot_general x1, matrix products, on_device(): jnp.einsum('xfs,fsq->xfq', filled_lattice, phases, preferred_element_type...  10.1 us
  transfers between devices with their start and end apart: 2, of which 1 were waited for; matrix products, arithmetic and copies ran while one was open for 3% of the time, Pallas kernels for 0%

commit v1 on v0

v1 whole, which is shorter than its diff:
```python
import math

import jax
import jax.numpy as jnp
import ml_dtypes
import numpy as np
from jax import lax
from jax.experimental import pallas as pl
from jax.experimental.pallas import tpu as pltpu
from jax.sharding import PartitionSpec as P

NT = 2048
FREQUENCY_COUNT = 256
F0 = 8
RAY_PARAM_COUNT = 128
NREC = 512
RDIV = 16
SLAB_SLOTS = 48
ROWS = 3072
UNIT = 8
FREQ_DEV = 8
SLAB_DEV = 16
DEVICES = FREQ_DEV * SLAB_DEV
SLOTS = SLAB_SLOTS * SLAB_DEV
FB = FREQUENCY_COUNT // FREQ_DEV
VALUES = 2 * FREQUENCY_COUNT
SHOTS = UNIT * DEVICES
DFT_ROWS = 512
DFT_STEPS = ROWS // DFT_ROWS
LIMIT = 60 * 2**20


def dft_table():
    column = np.arange(VALUES)
    owner, within = column // (2 * FB), column % (2 * FB)
    bins = F0 + owner * FB + within % FB
    angle = (np.arange(NT)[:, None] * bins[None, :] % NT) * (2.0 * math.pi / NT)
    factor = 1.0 / math.sqrt(NT)
    table = np.where((within // FB == 0)[None, :], np.cos(angle), -np.sin(angle)) * factor
    return table.astype(np.float32).astype(ml_dtypes.bfloat16)


def spread_kernel(counts, starts, traces, table, rec_slot, out, spectra, placed):
    step = pl.program_id(0)

    @pl.when(step == 0)
    def _():
        spectra[ROWS:, :] = jnp.zeros((spectra.shape[0] - ROWS, VALUES), jnp.bfloat16)

    @pl.when(step < DFT_STEPS)
    def _():
        rows = pl.multiple_of(step * DFT_ROWS, DFT_ROWS)
        spectra[pl.ds(rows, DFT_ROWS), :] = jnp.dot(
            traces[...], table[...], preferred_element_type=jnp.float32
        ).astype(jnp.bfloat16)

    @pl.when(step >= DFT_STEPS)
    def _():
        quarter = step - DFT_STEPS
        for half in range(2):
            shot = half * 4 + quarter
            begin = jnp.int32(0)
            for k in range(UNIT):
                begin = begin + jnp.where(k < shot, counts[0, k], 0)
            count = counts[0, shot]
            start = starts[shot]
            base = pl.multiple_of((begin // 16) * 16, 16)
            skip = begin - base
            shift = lax.rem(skip - start + NREC, NREC)
            slots = pltpu.roll(rec_slot[...], shift, 1)[:1]

            def place(depth):
                names = slots if depth <= NREC else jnp.concatenate([slots, slots[:, : depth - NREC]], axis=1)
                names = names[:, :depth]
                lane = lax.broadcasted_iota(jnp.int32, (1, depth), 1) - skip
                names = jnp.where((lane >= 0) & (lane < count), names, -1)
                onehot = (lax.broadcasted_iota(jnp.int32, (SLOTS, depth), 0) == names).astype(jnp.float32)
                placed[half] = jnp.dot(
                    onehot.astype(jnp.bfloat16),
                    spectra[pl.ds(base, depth), :],
                    preferred_element_type=jnp.float32,
                )

            small = skip + count <= NREC

            @pl.when(small)
            def _():
                place(NREC)

            @pl.when(jnp.logical_not(small))
            def _():
                place(NREC + 256)

        low = lax.broadcasted_iota(jnp.int32, (SLOTS, 128), 1) < 64
        for pair in range(FREQ_DEV // 2):
            first = placed[0, :, pair * 128 : pair * 128 + 128]
            second = placed[1, :, pair * 128 : pair * 128 + 128]
            even = jnp.where(low, first, pltpu.roll(second, 64, 1)).astype(jnp.bfloat16)
            odd = jnp.where(low, pltpu.roll(first, 64, 1), second).astype(jnp.bfloat16)
            own = 2 * pair * SLAB_DEV
            out[own : own + SLAB_DEV, 0] = even.reshape(SLAB_DEV, SLAB_SLOTS, 128)
            out[own + SLAB_DEV : own + 2 * SLAB_DEV, 0] = odd.reshape(SLAB_DEV, SLAB_SLOTS, 128)


def spread(traces, counts, starts, rec_slot):
    return pl.pallas_call(
        spread_kernel,
        grid=(DFT_STEPS + 4,),
        in_specs=[
            pl.BlockSpec(memory_space=pltpu.SMEM),
            pl.BlockSpec(memory_space=pltpu.SMEM),
            pl.BlockSpec((DFT_ROWS, NT), lambda i: (jnp.minimum(i, DFT_STEPS - 1), 0)),
            pl.BlockSpec((NT, VALUES), lambda i: (0, 0)),
            pl.BlockSpec((8, NREC), lambda i: (0, 0)),
        ],
        out_specs=pl.BlockSpec(
            (DEVICES, 1, SLAB_SLOTS, 128), lambda i: (0, jnp.maximum(i - DFT_STEPS, 0), 0, 0)
        ),
        out_shape=jax.ShapeDtypeStruct((DEVICES, 4, SLAB_SLOTS, 128), jnp.bfloat16),
        scratch_shapes=[
            pltpu.VMEM((ROWS + 768, VALUES), jnp.bfloat16),
            pltpu.VMEM((2, SLOTS, VALUES), jnp.float32),
        ],
        compiler_params=pltpu.CompilerParams(vmem_limit_bytes=LIMIT),
    )(counts, starts, traces, jnp.asarray(dft_table()), jnp.broadcast_to(rec_slot[None, :], (8, NREC)))


PHASE_ROWS = 128


def phase_kernel(first_bin, positions, out):
    period = NT * RDIV
    unit = 2.0 * math.pi / period
    scale = 1.0 / math.sqrt(SHOTS)
    tile = 16
    ray = lax.broadcasted_iota(jnp.int32, (tile, RAY_PARAM_COUNT), 1) - RAY_PARAM_COUNT // 2

    def turn(k):
        centred = ((k + period // 2) & (period - 1)) - period // 2
        angle = centred.astype(jnp.float32) * unit
        return jnp.cos(angle), jnp.sin(angle)

    def body(t, carry):
        rows = pl.multiple_of(t * tile, tile)
        delay = positions[pl.ds(rows, tile), :] * ray
        step_cos, step_sin = turn(delay)
        c, s = turn(delay * first_bin[0])
        c, s = c * scale, s * scale
        for f in range(FB):
            out[f, pl.ds(rows, tile), :RAY_PARAM_COUNT] = c.astype(jnp.bfloat16)
            out[f, pl.ds(rows, tile), RAY_PARAM_COUNT:] = s.astype(jnp.bfloat16)
            c, s = c * step_cos - s * step_sin, s * step_cos + c * step_sin
        return carry

    lax.fori_loop(0, PHASE_ROWS // tile, body, 0)


def phases(first_bin, positions):
    return pl.pallas_call(
        phase_kernel,
        grid=(SHOTS // PHASE_ROWS,),
        in_specs=[
            pl.BlockSpec(memory_space=pltpu.SMEM),
            pl.BlockSpec((PHASE_ROWS, RAY_PARAM_COUNT), lambda i: (i, 0)),
        ],
        out_specs=pl.BlockSpec((FB, PHASE_ROWS, 2 * RAY_PARAM_COUNT), lambda i: (0, i, 0)),
        out_shape=jax.ShapeDtypeStruct((FB, SHOTS, 2 * RAY_PARAM_COUNT), jnp.bfloat16),
        compiler_params=pltpu.CompilerParams(vmem_limit_bytes=LIMIT),
    )(first_bin, positions)


PART = 16
TURN_STEPS = 4 * (SLAB_SLOTS // PART)
GROUP = 4
LANES = 2 * SLAB_SLOTS


def encode_kernel(blocks, table, out, wide, lattice, encoded):
    step = pl.program_id(0)

    @pl.when(step < TURN_STEPS)
    def _():
        quarter = step // (SLAB_SLOTS // PART)
        part = lax.rem(step, SLAB_SLOTS // PART)
        wide[...] = blocks[...].reshape(DEVICES * PART, 128).astype(jnp.float32)
        eye = (
            lax.broadcasted_iota(jnp.int32, (128, 128), 0) == lax.broadcasted_iota(jnp.int32, (128, 128), 1)
        ).astype(jnp.float32).astype(jnp.bfloat16)
        for s in range(PART):
            rows = wide[pl.ds(s, DEVICES, stride=PART), :].astype(jnp.bfloat16)
            turned = lax.dot_general(
                eye, rows, (((1,), (1,)), ((), ())), preferred_element_type=jnp.float32
            )
            for half in range(2):
                for c in range(2):
                    at = half * 64 + c * FB
                    lattice[
                        half * 4 + quarter, pl.ds(c * SLAB_SLOTS + part * PART + s, FB, stride=LANES), :
                    ] = turned[at : at + FB, :]

    @pl.when(step >= TURN_STEPS)
    def _():
        group = step - TURN_STEPS
        for k in range(GROUP):
            f = group * GROUP + k
            at = pl.multiple_of(f * LANES, LANES)
            rows = jnp.concatenate(
                [lattice[o, pl.ds(at, LANES), :].astype(jnp.bfloat16) for o in range(UNIT)], axis=1
            )
            both = jnp.dot(rows, table[k], preferred_element_type=jnp.float32)
            re, im = both[:SLAB_SLOTS], both[SLAB_SLOTS:]
            n = RAY_PARAM_COUNT
            encoded[0, pl.ds(f, SLAB_SLOTS, stride=FB), :] = re[:, :n] + im[:, n:]
            encoded[1, pl.ds(f, SLAB_SLOTS, stride=FB), :] = im[:, :n] - re[:, n:]

    @pl.when(step == pl.num_programs(0) - 1)
    def _():
        for h in range(2):
            out[:, :, h * RAY_PARAM_COUNT : (h + 1) * RAY_PARAM_COUNT] = (
                encoded[h].reshape(SLAB_SLOTS, FB, RAY_PARAM_COUNT).astype(jnp.bfloat16)
            )


def encode(blocks, table):
    parts = SLAB_SLOTS // PART
    return pl.pallas_call(
        encode_kernel,
        grid=(TURN_STEPS + FB // GROUP,),
        in_specs=[
            pl.BlockSpec(
                (DEVICES, 1, PART, 128),
                lambda i: (0, jnp.minimum(i, TURN_STEPS - 1) // parts, lax.rem(jnp.minimum(i, TURN_STEPS - 1), parts), 0),
            ),
            pl.BlockSpec(
                (GROUP, SHOTS, 2 * RAY_PARAM_COUNT), lambda i: (jnp.maximum(i - TURN_STEPS, 0), 0, 0)
            ),
        ],
        out_specs=pl.BlockSpec((SLAB_SLOTS, FB, 2 * RAY_PARAM_COUNT), lambda i: (0, 0, 0)),
        out_shape=jax.ShapeDtypeStruct((SLAB_SLOTS, FB, 2 * RAY_PARAM_COUNT), jnp.bfloat16),
        scratch_shapes=[
            pltpu.VMEM((DEVICES * PART, 128), jnp.float32),
            pltpu.VMEM((UNIT, FB * LANES, 128), jnp.float32),
            pltpu.VMEM((2, SLAB_SLOTS * FB, RAY_PARAM_COUNT), jnp.float32),
        ],
        compiler_params=pltpu.CompilerParams(vmem_limit_bytes=LIMIT),
    )(blocks, table)


def on_device(traces, trace_counts, aperture_start, shot_position, rec_slot):
    blocks = spread(traces, trace_counts, aperture_start, rec_slot)
    blocks, own_positions = lax.optimization_barrier((blocks, shot_position))
    received = lax.all_to_all(blocks, ("freq", "slab"), split_axis=0, concat_axis=0, tiled=True)
    positions = lax.all_gather(own_positions, ("freq", "slab"), axis=0, tiled=True)
    ordered = positions.reshape(DEVICES, UNIT).T.reshape(SHOTS, 1)
    first_bin = (F0 + lax.axis_index("freq") * FB).astype(jnp.int32).reshape(1)
    table = phases(first_bin, jnp.broadcast_to(ordered, (SHOTS, RAY_PARAM_COUNT)))
    return encode(received, table)


def solution(mesh):
    return jax.shard_map(
        on_device,
        mesh=mesh,
        in_specs=(
            P(("freq", "slab"), None),
            P(("freq", "slab"), None),
            P(("freq", "slab")),
            P(("freq", "slab")),
            P(),
        ),
        out_specs=P("slab", "freq", None),
        check_vma=False,
    )
```

time: 434 us -> 207 us (0.48)
  local copies, waits for them, and re-layouts: 163 us -> 2.69 us
  waiting for transfers between devices: 155 us -> 0.01 us
  blocking collectives: 37.4 us -> 133 us
  Pallas kernels: 0 us -> 59.3 us
  matrix products: 44.6 us -> 0 us
  between operations: 14.2 us -> 0.04 us
  other arithmetic: 12.9 us -> 0 us
  starting transfers between devices: 6.13 us -> 12.2 us
    reduce_scatter x1 -> x0, waiting for transfers between devices: 155 us -> none  [on_device(): lax.psum_scatter(jnp.einsum('xfs,fsq->xfq', filled_lattice, phases, prefe...]
    gather x2 -> x0, local copies, waits for them, and re-layouts: 122 us -> none  [slot_grid(): picked = jnp.take(owned_spectra, picks.reshape(-1), axis=1)]
    unnamed x1, blocking collectives: 37.4 us -> 133 us
    pallas_call x0 -> x3, Pallas kernels: none -> 59.3 us  [the longest x1 27.1 us: encode(): pl.pallas_call(encode_kernel, grid=(TURN_STEPS + FB // GROUP,), in_specs=...]
    dot_general x3 -> x0, matrix products: 44.6 us -> none  [the longest x1 28.7 us: frequency_spectra(): lax.dot_general(transform, traces, (((0,), (1,)), ((), ())), preferred_el...]
    transpose x1, local copies, waits for them, and re-layouts: 25.1 us -> 0.05 us  [on_device(): ordered = positions.reshape(DEVICES, UNIT).T.reshape(SHOTS, 1)]
    convert_element_type x2 -> x0, other arithmetic: 6.99 us -> none  [the longest x1 4.58 us: phase_blocks(): sine_part = (jnp.sin(angle_rad) * factor).astype(jnp.bfloat16)]
    all_to_all x1 -> x0, local copies, waits for them, and re-layouts: 6.59 us -> none  [on_device(): lax.all_to_all(spectra, 'freq', split_axis=0, concat_axis=1, tiled=True)]
  transfers between devices with their start and end apart: 2 -> 1, of which waited for: 1 -> 0; matrix products, arithmetic and copies ran while one was open for 3% -> 1% of each run, Pallas kernels for 0% -> 6%
where the time goes in v1:
time: 207 us
  blocking collectives  133 us (64%)
  Pallas kernels  59.3 us (29%)
  starting transfers between devices  12.2 us (6%)
  local copies, waits for them, and re-layouts  2.69 us (1%)
    unnamed x1, blocking collectives  133 us
    pallas_call x1, Pallas kernels, encode(): pl.pallas_call(encode_kernel, grid=(TURN_STEPS + FB // GROUP,), in_specs=...  27.1 us
    pallas_call x1, Pallas kernels, spread(): pl.pallas_call(spread_kernel, grid=(DFT_STEPS + 4,), in_specs=[pl.BlockSp...  19.6 us
    pallas_call x1, Pallas kernels, phases(): pl.pallas_call(phase_kernel, grid=(SHOTS // PHASE_ROWS,), in_specs=[pl.Bl...  12.6 us
    all_to_all x1, starting transfers between devices, on_device(): lax.all_to_all(blocks, ('freq', 'slab'), split_axis=0, concat_axis=0, til...  12.2 us
  transfers between devices with their start and end apart: 1, of which 0 were waited for; matrix products, arithmetic and copies ran while one was open for 1% of the time, Pallas kernels for 6%

profile of v1, /device:TPU:1, one launch (start us, length us, event | category | flops | bytes accessed | tf_op | source)
XLA Modules:
  0.0 206.8 jit_solution(4303413391304100900)
XLA Ops:
  0.0 1.3 broadcast_in_dim.6.rec_slot
  1.3 19.6 %shard_map.64 = bf16[128,4,48,128]{3,2,1,0:T(8,128)(2,1)} custom-call(s32[1,8]{1,0:T(1,128)} %counts.1, s32[8]{0:T(128)} %starts.1, bf16[3072,2048]{1,0:T(8,128)(2,1)} %traces.1, bf16[2048,512]{1,0:T(8,128)(2,1)} %constant.12.clone.table, s32[8,512]{1,0:T(8,128)} %broadcast_in_dim.6.rec_slot), custom_call_target="tpu_custom_call" | custom-call | tf_op jit(solution)/shard_map/pallas_call | solution.py:106
  20.9 0.0 copy-start
  20.9 12.2 %all-to-all-start = ((bf16[128,4,48,128]{3,2,1,0:T(8,128)(2,1)}), bf16[128,4,48,128]{3,2,1,0:T(8,128)(2,1)}, u32[]{:S(2)}, u32[]{:S(2)}) async-start(bf16[128,4,48,128]{3,2,1,0:T(8,128)(2,1)} %shard_map.64), calls=%async_computation | async-start | bytes 12582912 | tf_op jit(solution)/shard_map/all_to_all | solution.py:252
  33.1 0.0 copy-done
  33.1 0.2 dynamic-update-slice
  33.4 132.6 %all-reduce = s32[1024]{0:T(1024)S(1)} all-reduce(s32[1024]{0:T(1024)S(1)} %dynamic-update-slice), channel_id=1, replica_groups=mesh['freq'=8,'slab'=16] {'freq','slab'}, use_global_device_ids=true, to_apply=%add | all-reduce | flops 1024 | bytes 8192
  166.0 0.1 reshape.10
  166.1 1.0 broadcast_in_dim.15.positions
  167.1 12.6 %shard_map.65.table = bf16[32,1024,256]{2,1,0:T(8,128)(2,1)} custom-call(s32[1]{0:T(128)} %bitcast.first_bin, s32[1024,128]{1,0:T(8,128)} %broadcast_in_dim.15.positions), custom_call_target="tpu_custom_call" | custom-call | tf_op jit(solution)/shard_map/pallas_call | solution.py:159
  179.7 0.0 all-to-all-done.blocks
  179.7 27.1 %shard_map.66 = bf16[48,32,256]{2,1,0:T(8,128)(2,1)} custom-call(bf16[128,4,48,128]{3,2,1,0:T(8,128)(2,1)} %all-to-all-done.blocks, bf16[32,1024,256]{2,1,0:T(8,128)(2,1)} %shard_map.65.table), custom_call_target="tpu_custom_call" | custom-call | tf_op jit(solution)/shard_map/pallas_call | solution.py:226
  (2 shorter events, 0.1 us)
Async XLA Ops:
  20.9 12.2 %copy-start = (s32[8]{0:T(128)S(1)}, s32[8]{0:T(128)}, u32[]{:S(2)}) copy-start(s32[8]{0:T(128)} %param.9) | copy-start | bytes 100
  20.9 158.8 %all-to-all-start = ((bf16[128,4,48,128]{3,2,1,0:T(8,128)(2,1)}), bf16[128,4,48,128]{3,2,1,0:T(8,128)(2,1)}, u32[]{:S(2)}, u32[]{:S(2)}) async-start(bf16[128,4,48,128]{3,2,1,0:T(8,128)(2,1)} %shard_map.64), calls=%async_computation | async-start | bytes 12582912 | tf_op jit(solution)/shard_map/all_to_all | solution.py:252

commit v2 on v1

v2 whole, which is shorter than its diff:
```python
import math

import jax
import jax.numpy as jnp
import ml_dtypes
import numpy as np
from jax import lax
from jax.experimental import pallas as pl
from jax.experimental.pallas import tpu as pltpu
from jax.sharding import PartitionSpec as P

NT = 2048
FREQUENCY_COUNT = 256
F0 = 8
RAY_PARAM_COUNT = 128
NREC = 512
RDIV = 16
SLAB_SLOTS = 48
ROWS = 3072
UNIT = 8
FREQ_DEV = 8
SLAB_DEV = 16
DEVICES = FREQ_DEV * SLAB_DEV
SLOTS = SLAB_SLOTS * SLAB_DEV
FB = FREQUENCY_COUNT // FREQ_DEV
PASSES = 2
FC = FB // PASSES
VALUES = 2 * FC * FREQ_DEV
SPAN = 2 * FC
SIDE = 128 // SPAN
LAYERS = UNIT // SIDE
NOTE_ROWS = 8
SHOTS = UNIT * DEVICES
DFT_ROWS = 512
DFT_STEPS = ROWS // DFT_ROWS
LIMIT = 60 * 2**20


def dft_table(part):
    column = np.arange(VALUES)
    owner, within = column // SPAN, column % SPAN
    bins = F0 + owner * FB + part * FC + within % FC
    angle = (np.arange(NT)[:, None] * bins[None, :] % NT) * (2.0 * math.pi / NT)
    factor = 1.0 / math.sqrt(NT)
    table = np.where((within // FC == 0)[None, :], np.cos(angle), -np.sin(angle)) * factor
    return table.astype(np.float32).astype(ml_dtypes.bfloat16)


def spread_kernel(counts, starts, positions, traces, table, rec_slot, out, spectra, placed):
    step = pl.program_id(0)

    @pl.when(step == 0)
    def _():
        spectra[ROWS:, :] = jnp.zeros((spectra.shape[0] - ROWS, VALUES), jnp.bfloat16)

    @pl.when(step < DFT_STEPS)
    def _():
        rows = pl.multiple_of(step * DFT_ROWS, DFT_ROWS)
        spectra[pl.ds(rows, DFT_ROWS), :] = jnp.dot(
            traces[...], table[...], preferred_element_type=jnp.float32
        ).astype(jnp.bfloat16)

    @pl.when((step >= DFT_STEPS) & (step < DFT_STEPS + LAYERS))
    def _():
        layer = step - DFT_STEPS
        for side in range(SIDE):
            shot = layer * SIDE + side
            begin = jnp.int32(0)
            for k in range(UNIT):
                begin = begin + jnp.where(k < shot, counts[0, k], 0)
            count = counts[0, shot]
            start = starts[shot]
            base = pl.multiple_of((begin // 16) * 16, 16)
            skip = begin - base
            shift = lax.rem(skip - start + NREC, NREC)
            slots = pltpu.roll(rec_slot[...], shift, 1)[:1]

            def place(depth):
                names = slots if depth <= NREC else jnp.concatenate([slots, slots[:, : depth - NREC]], axis=1)
                names = names[:, :depth]
                lane = lax.broadcasted_iota(jnp.int32, (1, depth), 1) - skip
                names = jnp.where((lane >= 0) & (lane < count), names, -1)
                onehot = (lax.broadcasted_iota(jnp.int32, (SLOTS, depth), 0) == names).astype(jnp.float32)
                placed[side] = jnp.dot(
                    onehot.astype(jnp.bfloat16),
                    spectra[pl.ds(base, depth), :],
                    preferred_element_type=jnp.float32,
                )

            small = skip + count <= NREC

            @pl.when(small)
            def _():
                place(NREC)

            @pl.when(jnp.logical_not(small))
            def _():
                place(NREC + 256)

        group = lax.broadcasted_iota(jnp.int32, (SLOTS, 128), 1) // SPAN
        for tile in range(VALUES // 128):
            pieces = [placed[side, :, tile * 128 : tile * 128 + 128] for side in range(SIDE)]
            for k in range(SIDE):
                joined = pieces[k]
                for side in range(SIDE):
                    if side != k:
                        moved = pltpu.roll(pieces[side], (side - k) * SPAN % 128, 1)
                        joined = jnp.where(group == side, moved, joined)
                joined = jnp.where(group == k, pieces[k], joined).astype(jnp.bfloat16)
                owner = tile * SIDE + k
                out[owner * SLAB_DEV : (owner + 1) * SLAB_DEV] = joined.reshape(SLAB_DEV, SLAB_SLOTS, 128)

    @pl.when(step == DFT_STEPS + LAYERS)
    def _():
        lane = lax.broadcasted_iota(jnp.int32, (1, 16, 128), 2)
        note = jnp.zeros((1, 16, 128), jnp.int32)
        for k in range(UNIT):
            x = positions[k]
            note = jnp.where(lane == k, x // 64, note)
            note = jnp.where(lane == UNIT + k, lax.rem(x, 64), note)
        note = note.astype(jnp.float32).astype(jnp.bfloat16)
        out[:, :16] = jnp.broadcast_to(note, (DEVICES, 16, 128))


def spread(part, traces, counts, starts, positions, rec_slot):
    noted = part == 0
    return pl.pallas_call(
        spread_kernel,
        grid=(DFT_STEPS + LAYERS + noted,),
        in_specs=[
            pl.BlockSpec(memory_space=pltpu.SMEM),
            pl.BlockSpec(memory_space=pltpu.SMEM),
            pl.BlockSpec(memory_space=pltpu.SMEM),
            pl.BlockSpec((DFT_ROWS, NT), lambda i: (jnp.minimum(i, DFT_STEPS - 1), 0)),
            pl.BlockSpec((NT, VALUES), lambda i: (0, 0)),
            pl.BlockSpec((8, NREC), lambda i: (0, 0)),
        ],
        out_specs=pl.BlockSpec(
            (DEVICES, SLAB_SLOTS, 128), lambda i: (0, jnp.maximum(i - DFT_STEPS, 0), 0)
        ),
        out_shape=jax.ShapeDtypeStruct(
            (DEVICES, LAYERS * SLAB_SLOTS + NOTE_ROWS * noted, 128), jnp.bfloat16
        ),
        scratch_shapes=[
            pltpu.VMEM((ROWS + 768, VALUES), jnp.bfloat16),
            pltpu.VMEM((SIDE, SLOTS, VALUES), jnp.float32),
        ],
        compiler_params=pltpu.CompilerParams(vmem_limit_bytes=LIMIT),
    )(counts, starts, positions, traces, jnp.asarray(dft_table(part)), jnp.broadcast_to(rec_slot[None, :], (8, NREC)))


PHASE_ROWS = 128


def phase_kernel(first_bin, positions, out):
    period = NT * RDIV
    unit = 2.0 * math.pi / period
    scale = 1.0 / math.sqrt(SHOTS)
    tile = 16
    ray = lax.broadcasted_iota(jnp.int32, (tile, RAY_PARAM_COUNT), 1) - RAY_PARAM_COUNT // 2

    def turn(k):
        centred = ((k + period // 2) & (period - 1)) - period // 2
        angle = centred.astype(jnp.float32) * unit
        return jnp.cos(angle), jnp.sin(angle)

    def body(t, carry):
        rows = pl.multiple_of(t * tile, tile)
        delay = positions[pl.ds(rows, tile), :] * ray
        step_cos, step_sin = turn(delay)
        c, s = turn(delay * first_bin[0])
        c, s = c * scale, s * scale
        for f in range(FB):
            out[f, pl.ds(rows, tile), :RAY_PARAM_COUNT] = c.astype(jnp.bfloat16)
            out[f, pl.ds(rows, tile), RAY_PARAM_COUNT:] = s.astype(jnp.bfloat16)
            c, s = c * step_cos - s * step_sin, s * step_cos + c * step_sin
        return carry

    lax.fori_loop(0, PHASE_ROWS // tile, body, 0)


def phases(first_bin, positions):
    return pl.pallas_call(
        phase_kernel,
        grid=(SHOTS // PHASE_ROWS,),
        in_specs=[
            pl.BlockSpec(memory_space=pltpu.SMEM),
            pl.BlockSpec((PHASE_ROWS, RAY_PARAM_COUNT), lambda i: (i, 0)),
        ],
        out_specs=pl.BlockSpec((FB, PHASE_ROWS, 2 * RAY_PARAM_COUNT), lambda i: (0, i, 0)),
        out_shape=jax.ShapeDtypeStruct((FB, SHOTS, 2 * RAY_PARAM_COUNT), jnp.bfloat16),
        compiler_params=pltpu.CompilerParams(vmem_limit_bytes=LIMIT),
    )(first_bin, positions)


PART = 16
PARTS = SLAB_SLOTS // PART
TURN_STEPS = LAYERS * PARTS
GROUP = 4
LANES = 2 * SLAB_SLOTS


def encode_kernel(blocks, table, out, wide, lattice, encoded):
    step = pl.program_id(0)

    @pl.when(step < TURN_STEPS)
    def _():
        layer = step // PARTS
        part = lax.rem(step, PARTS)
        wide[...] = blocks[...].reshape(DEVICES * PART, 128).astype(jnp.float32)
        eye = (
            lax.broadcasted_iota(jnp.int32, (128, 128), 0) == lax.broadcasted_iota(jnp.int32, (128, 128), 1)
        ).astype(jnp.float32).astype(jnp.bfloat16)
        for s in range(PART):
            rows = wide[pl.ds(s, DEVICES, stride=PART), :].astype(jnp.bfloat16)
            turned = lax.dot_general(
                eye, rows, (((1,), (1,)), ((), ())), preferred_element_type=jnp.float32
            )
            for side in range(SIDE):
                for c in range(2):
                    at = side * SPAN + c * FC
                    lattice[
                        layer * SIDE + side, pl.ds(c * SLAB_SLOTS + part * PART + s, FC, stride=LANES), :
                    ] = turned[at : at + FC, :]

    @pl.when(step >= TURN_STEPS)
    def _():
        group = step - TURN_STEPS
        for k in range(GROUP):
            f = group * GROUP + k
            at = pl.multiple_of(f * LANES, LANES)
            rows = jnp.concatenate(
                [lattice[o, pl.ds(at, LANES), :].astype(jnp.bfloat16) for o in range(UNIT)], axis=1
            )
            both = jnp.dot(rows, table[k], preferred_element_type=jnp.float32)
            re, im = both[:SLAB_SLOTS], both[SLAB_SLOTS:]
            n = RAY_PARAM_COUNT
            encoded[0, pl.ds(f, SLAB_SLOTS, stride=FC), :] = re[:, :n] + im[:, n:]
            encoded[1, pl.ds(f, SLAB_SLOTS, stride=FC), :] = im[:, :n] - re[:, n:]

    @pl.when(step == pl.num_programs(0) - 1)
    def _():
        for h in range(2):
            out[:, :, h * RAY_PARAM_COUNT : (h + 1) * RAY_PARAM_COUNT] = (
                encoded[h].reshape(SLAB_SLOTS, FC, RAY_PARAM_COUNT).astype(jnp.bfloat16)
            )


def encode(part, blocks, table):
    return pl.pallas_call(
        encode_kernel,
        grid=(TURN_STEPS + FC // GROUP,),
        in_specs=[
            pl.BlockSpec((DEVICES, PART, 128), lambda i: (0, jnp.minimum(i, TURN_STEPS - 1), 0)),
            pl.BlockSpec(
                (GROUP, SHOTS, 2 * RAY_PARAM_COUNT),
                lambda i: (part * (FC // GROUP) + jnp.maximum(i - TURN_STEPS, 0), 0, 0),
            ),
        ],
        out_specs=pl.BlockSpec((SLAB_SLOTS, FC, 2 * RAY_PARAM_COUNT), lambda i: (0, 0, 0)),
        out_shape=jax.ShapeDtypeStruct((SLAB_SLOTS, FC, 2 * RAY_PARAM_COUNT), jnp.bfloat16),
        scratch_shapes=[
            pltpu.VMEM((DEVICES * PART, 128), jnp.float32),
            pltpu.VMEM((UNIT, FC * LANES, 128), jnp.float32),
            pltpu.VMEM((2, SLAB_SLOTS * FC, RAY_PARAM_COUNT), jnp.float32),
        ],
        compiler_params=pltpu.CompilerParams(vmem_limit_bytes=LIMIT),
    )(blocks, table)


def on_device(traces, trace_counts, aperture_start, shot_position, rec_slot):
    own = (trace_counts, aperture_start, shot_position, rec_slot)
    everyone = ("freq", "slab")
    first = lax.all_to_all(spread(0, traces, *own), everyone, split_axis=0, concat_axis=0, tiled=True)
    second = lax.all_to_all(spread(1, traces, *own), everyone, split_axis=0, concat_axis=0, tiled=True)
    note = first[:, LAYERS * SLAB_SLOTS, : 2 * UNIT].astype(jnp.int32)
    positions = note[:, :UNIT] * 64 + note[:, UNIT:]
    ordered = positions.T.reshape(SHOTS, 1)
    first_bin = (F0 + lax.axis_index("freq") * FB).astype(jnp.int32).reshape(1)
    table = phases(first_bin, jnp.broadcast_to(ordered, (SHOTS, RAY_PARAM_COUNT)))
    return jnp.concatenate([encode(0, first, table), encode(1, second, table)], axis=1)


def solution(mesh):
    return jax.shard_map(
        on_device,
        mesh=mesh,
        in_specs=(
            P(("freq", "slab"), None),
            P(("freq", "slab"), None),
            P(("freq", "slab")),
            P(("freq", "slab")),
            P(),
        ),
        out_specs=P("slab", "freq", None),
        check_vma=False,
    )
```

time: 207 us -> 136 us (0.66)
  blocking collectives: 133 us -> 0 us
  waiting for transfers between devices: 0.01 us -> 40.4 us
  Pallas kernels: 59.3 us -> 73.2 us
  starting transfers between devices: 12.2 us -> 17.2 us
  other arithmetic: 0 us -> 2.09 us
    unnamed x1 -> x0, blocking collectives: 133 us -> none
    all_to_all x1 -> x2, waiting for transfers between devices: 0.01 us -> 40.4 us  [the longest x1 27 us: on_device(): lax.all_to_all(spread(0, traces, *own), everyone, split_axis=0, concat_ax...]
    pallas_call x2 -> x4, Pallas kernels: 46.7 us -> 60.7 us  [the longest x2 33.5 us: spread(): pl.pallas_call(spread_kernel, grid=(DFT_STEPS + LAYERS + noted,), in_spec...]
    all_to_all x1 -> x2, starting transfers between devices: 12.2 us -> 17.2 us  [the longest x1 11.5 us: on_device(): lax.all_to_all(spread(0, traces, *own), everyone, split_axis=0, concat_ax...]
  transfers between devices with their start and end apart: 1 -> 2, of which waited for: 0 -> 2; matrix products, arithmetic and copies ran while one was open for 1% -> 1% of each run, Pallas kernels for 6% -> 32%
where the time goes in v2:
time: 136 us; the launch traced here: 135 us
  Pallas kernels  73.2 us (54%)
  waiting for transfers between devices  40.4 us (30%)
  starting transfers between devices  17.2 us (13%)
  local copies, waits for them, and re-layouts  2.36 us (2%)
  other arithmetic  2.09 us (2%)
    pallas_call x2, Pallas kernels, spread(): pl.pallas_call(spread_kernel, grid=(DFT_STEPS + LAYERS + noted,), in_spec...  33.5 us
    pallas_call x2, Pallas kernels, encode(): pl.pallas_call(encode_kernel, grid=(TURN_STEPS + FC // GROUP,), in_specs=...  27.2 us
    all_to_all x1, waiting for transfers between devices, on_device(): lax.all_to_all(spread(0, traces, *own), everyone, split_axis=0, concat_ax...  27 us
    all_to_all x1, waiting for transfers between devices, on_device(): lax.all_to_all(spread(1, traces, *own), everyone, split_axis=0, concat_ax...  13.4 us
    pallas_call x1, Pallas kernels, phases(): pl.pallas_call(phase_kernel, grid=(SHOTS // PHASE_ROWS,), in_specs=[pl.Bl...  12.5 us
    all_to_all x1, starting transfers between devices, on_device(): lax.all_to_all(spread(0, traces, *own), everyone, split_axis=0, concat_ax...  11.5 us
    all_to_all x1, starting transfers between devices, on_device(): lax.all_to_all(spread(1, traces, *own), everyone, split_axis=0, concat_ax...  5.71 us
  transfers between devices with their start and end apart: 2, of which 2 were waited for; matrix products, arithmetic and copies ran while one was open for 1% of the time, Pallas kernels for 32%

profile of v2, /device:TPU:1, one launch (start us, length us, event | category | flops | bytes accessed | tf_op | source)
XLA Modules:
  0.0 135.3 jit_solution(4363512458798621032)
XLA Ops:
  0.0 1.3 broadcast_in_dim.6.rec_slot
  1.3 16.8 %shard_map.73 = bf16[128,104,128]{2,1,0:T(8,128)(2,1)} custom-call(s32[1,8]{1,0:T(1,128)} %counts.3, s32[8]{0:T(128)} %starts.3, s32[8]{0:T(128)} %positions.3, bf16[3072,2048]{1,0:T(8,128)(2,1)} %traces.3, bf16[2048,256]{1,0:T(8,128)(2,1)} %constant.16.clone.table, s32[8,512]{1,0:T(8,128)} %broadcast_in_dim.6.rec_slot), custom_call_target="tpu_custom_call" | custom-call | tf_op jit(solution)/shard_map/pallas_call | solution.py:127
  18.1 11.5 %all-to-all-start = ((bf16[128,104,128]{2,1,0:T(8,128)(2,1)}), bf16[128,104,128]{2,1,0:T(8,128)(2,1)S(1)}, u32[]{:S(2)}, u32[]{:S(2)}) async-start(bf16[128,104,128]{2,1,0:T(8,128)(2,1)} %shard_map.73), calls=%async_computation | async-start | bytes 6815744 | tf_op jit(solution)/shard_map/all_to_all | solution.py:274
  29.6 16.7 %shard_map.76 = bf16[128,96,128]{2,1,0:T(8,128)(2,1)} custom-call(s32[1,8]{1,0:T(1,128)} %counts.3, s32[8]{0:T(128)} %starts.3, s32[8]{0:T(128)} %positions.3, bf16[3072,2048]{1,0:T(8,128)(2,1)} %traces.3, bf16[2048,256]{1,0:T(8,128)(2,1)} %constant.17.clone.table, s32[8,512]{1,0:T(8,128)} %broadcast_in_dim.6.rec_slot), custom_call_target="tpu_custom_call" | custom-call | tf_op jit(solution)/shard_map/pallas_call | solution.py:127
  46.3 27.0 %all-to-all-done.blocks = bf16[128,104,128]{2,1,0:T(8,128)(2,1)S(1)} async-done(((bf16[128,104,128]{2,1,0:T(8,128)(2,1)}), bf16[128,104,128]{2,1,0:T(8,128)(2,1)S(1)}, u32[]{:S(2)}, u32[]{:S(2)}) %all-to-all-start) | async-done | bytes 3407904 | tf_op jit(solution)/shard_map/all_to_all | solution.py:274
  73.3 0.0 copy-start
  73.3 5.7 %all-to-all-start.1 = ((bf16[128,96,128]{2,1,0:T(8,128)(2,1)}), bf16[128,96,128]{2,1,0:T(8,128)(2,1)}, u32[]{:S(2)}, u32[]{:S(2)}) async-start(bf16[128,96,128]{2,1,0:T(8,128)(2,1)} %shard_map.76), calls=%async_computation.1 | async-start | bytes 6291456 | tf_op jit(solution)/shard_map/all_to_all | solution.py:275
  79.0 0.1 slice_convert_fusion
  79.1 0.1 fusion
  79.2 1.0 broadcast_in_dim.8.positions
  80.3 0.0 copy-done
  80.3 12.5 %shard_map.74.table = bf16[32,1024,256]{2,1,0:T(8,128)(2,1)} custom-call(s32[1]{0:T(128)} %bitcast.first_bin, s32[1024,128]{1,0:T(8,128)} %broadcast_in_dim.8.positions), custom_call_target="tpu_custom_call" | custom-call | tf_op jit(solution)/shard_map/pallas_call | solution.py:183
  92.8 13.6 %shard_map.75 = bf16[48,16,256]{2,1,0:T(8,128)(2,1)} custom-call(bf16[128,104,128]{2,1,0:T(8,128)(2,1)} %copy-done, bf16[32,1024,256]{2,1,0:T(8,128)(2,1)} %shard_map.74.table), custom_call_target="tpu_custom_call" | custom-call | tf_op jit(solution)/shard_map/pallas_call | solution.py:250
  106.3 0.0 copy-start.1
  106.3 13.4 %all-to-all-done.1.blocks = bf16[128,96,128]{2,1,0:T(8,128)(2,1)} async-done(((bf16[128,96,128]{2,1,0:T(8,128)(2,1)}), bf16[128,96,128]{2,1,0:T(8,128)(2,1)}, u32[]{:S(2)}, u32[]{:S(2)}) %all-to-all-start.1) | async-done | bytes 3145760 | tf_op jit(solution)/shard_map/all_to_all | solution.py:275
  119.7 13.6 %shard_map.77 = bf16[48,16,256]{2,1,0:T(8,128)(2,1)} custom-call(bf16[128,96,128]{2,1,0:T(8,128)(2,1)} %all-to-all-done.1.blocks, bf16[32,1024,256]{2,1,0:T(8,128)(2,1)} %shard_map.74.table), custom_call_target="tpu_custom_call" | custom-call | tf_op jit(solution)/shard_map/pallas_call | solution.py:250
  133.3 0.0 copy-done.1
  133.3 2.0 %pad_maximum_fusion = bf16[48,32,256]{2,1,0:T(8,128)(2,1)} fusion(bf16[48,16,256]{2,1,0:T(8,128)(2,1)} %shard_map.77, bf16[48,16,256]{2,1,0:T(8,128)(2,1)S(1)} %copy-done.1), kind=kLoop, calls=%fused_computation | loop fusion | flops 1572864 | bytes 1572864 | tf_op jit(solution)/shard_map/concatenate | solution.py:281
  (1 shorter events, 0.0 us)
Async XLA Ops:
  18.1 55.2 %all-to-all-start = ((bf16[128,104,128]{2,1,0:T(8,128)(2,1)}), bf16[128,104,128]{2,1,0:T(8,128)(2,1)S(1)}, u32[]{:S(2)}, u32[]{:S(2)}) async-start(bf16[128,104,128]{2,1,0:T(8,128)(2,1)} %shard_map.73), calls=%async_computation | async-start | bytes 6815744 | tf_op jit(solution)/shard_map/all_to_all | solution.py:274
  73.3 6.9 %copy-start = (bf16[128,104,128]{2,1,0:T(8,128)(2,1)}, bf16[128,104,128]{2,1,0:T(8,128)(2,1)S(1)}, u32[]{:S(2)}) copy-start(bf16[128,104,128]{2,1,0:T(8,128)(2,1)S(1)} %all-to-all-done.blocks) | copy-start | bytes 10223620
  73.3 46.4 %all-to-all-start.1 = ((bf16[128,96,128]{2,1,0:T(8,128)(2,1)}), bf16[128,96,128]{2,1,0:T(8,128)(2,1)}, u32[]{:S(2)}, u32[]{:S(2)}) async-start(bf16[128,96,128]{2,1,0:T(8,128)(2,1)} %shard_map.76), calls=%async_computation.1 | async-start | bytes 6291456 | tf_op jit(solution)/shard_map/all_to_all | solution.py:275
  106.3 27.0 %copy-start.1 = (bf16[48,16,256]{2,1,0:T(8,128)(2,1)S(1)}, bf16[48,16,256]{2,1,0:T(8,128)(2,1)}, u32[]{:S(2)}) copy-start(bf16[48,16,256]{2,1,0:T(8,128)(2,1)} %shard_map.75) | copy-start | bytes 1179652

commit v3 on v2

v3 whole, which is shorter than its diff:
```python
import math

import jax
import jax.numpy as jnp
import ml_dtypes
import numpy as np
from jax import lax
from jax.experimental import pallas as pl
from jax.experimental.pallas import tpu as pltpu
from jax.sharding import PartitionSpec as P

NT = 2048
FREQUENCY_COUNT = 256
F0 = 8
RAY_PARAM_COUNT = 128
NREC = 512
RDIV = 16
SLAB_SLOTS = 48
ROWS = 3072
UNIT = 8
FREQ_DEV = 8
SLAB_DEV = 16
DEVICES = FREQ_DEV * SLAB_DEV
SLOTS = SLAB_SLOTS * SLAB_DEV
FB = FREQUENCY_COUNT // FREQ_DEV
PASSES = 2
FC = FB // PASSES
VALUES = 2 * FC * FREQ_DEV
SPAN = 2 * FC
SIDE = 128 // SPAN
LAYERS = UNIT // SIDE
NOTE_ROWS = 8
SHOTS = UNIT * DEVICES
DFT_ROWS = 512
DFT_STEPS = ROWS // DFT_ROWS
LIMIT = 60 * 2**20


def dft_table(part):
    column = np.arange(VALUES)
    owner, within = column // SPAN, column % SPAN
    bins = F0 + owner * FB + part * FC + within % FC
    angle = (np.arange(NT)[:, None] * bins[None, :] % NT) * (2.0 * math.pi / NT)
    factor = 1.0 / math.sqrt(NT)
    table = np.where((within // FC == 0)[None, :], np.cos(angle), -np.sin(angle)) * factor
    return table.astype(np.float32).astype(ml_dtypes.bfloat16)


def spread_kernel(counts, starts, positions, rec_slot, traces, table, out, rows_in, factors, spectra, placed, stage, in_sem, out_sem):
    def rows_copy(i):
        at = pl.ds(pl.multiple_of(i * DFT_ROWS, DFT_ROWS), DFT_ROWS)
        return pltpu.make_async_copy(traces.at[at], rows_in.at[at], in_sem.at[i])

    def owner_copy(owner):
        at = pl.ds(owner * SLAB_DEV, SLAB_DEV)
        return pltpu.make_async_copy(stage.at[at], out.at[at], out_sem.at[owner])

    table_copy = pltpu.make_async_copy(table, factors, in_sem.at[DFT_STEPS])
    table_copy.start()
    for i in range(DFT_STEPS):
        rows_copy(i).start()
    spectra[...] = jnp.zeros(spectra.shape, jnp.bfloat16)
    if stage.shape[1] > LAYERS * SLAB_SLOTS:
        lane = lax.broadcasted_iota(jnp.int32, (1, NOTE_ROWS, 128), 2)
        note = jnp.zeros((1, NOTE_ROWS, 128), jnp.int32)
        for k in range(UNIT):
            x = positions[k]
            note = jnp.where(lane == k, x // 64, note)
            note = jnp.where(lane == UNIT + k, lax.rem(x, 64), note)
        note = note.astype(jnp.float32).astype(jnp.bfloat16)
        stage[:, LAYERS * SLAB_SLOTS :] = jnp.broadcast_to(note, (DEVICES, NOTE_ROWS, 128))
    table_copy.wait()
    group = lax.broadcasted_iota(jnp.int32, (SLOTS, 128), 1) // SPAN

    def join(layer):
        at = pl.ds(pl.multiple_of(layer * SLAB_SLOTS, 16), SLAB_SLOTS)
        for tile in range(VALUES // 128):
            pieces = [placed[side, :, tile * 128 : tile * 128 + 128] for side in range(SIDE)]
            for k in range(SIDE):
                joined = pieces[(SIDE - 1 - k) % SIDE]
                for g in range(SIDE - 1):
                    joined = jnp.where(group == g, pieces[(g - k) % SIDE], joined)
                owner = tile * SIDE + k
                stage[owner * SLAB_DEV : (owner + 1) * SLAB_DEV, at] = joined.astype(jnp.bfloat16).reshape(
                    SLAB_DEV, SLAB_SLOTS, 128
                )

                @pl.when(layer == LAYERS - 1)
                def _():
                    owner_copy(owner).start()

    def place(carry):
        shot, begin = carry
        side = lax.rem(shot, SIDE)
        count = counts[0, shot]
        base = pl.multiple_of((begin // 16) * 16, 16)
        skip = begin - base
        shift = lax.rem(skip - starts[shot] + NREC, NREC)
        slots = pltpu.roll(jnp.broadcast_to(rec_slot[...], (8, NREC)), shift, 1)[:1]

        def product(depth):
            names = slots if depth == NREC else jnp.concatenate([slots, slots[:, : depth - NREC]], axis=1)
            lane = lax.broadcasted_iota(jnp.int32, (1, depth), 1) - skip
            names = jnp.where((lane >= 0) & (lane < count), names, -1)
            onehot = (lax.broadcasted_iota(jnp.int32, (SLOTS, depth), 0) == names).astype(jnp.float32)
            found = jnp.dot(
                onehot.astype(jnp.bfloat16),
                spectra[pl.ds(base, depth), :],
                preferred_element_type=jnp.float32,
            )
            for tile in range(VALUES // 128):
                lanes = slice(tile * 128, tile * 128 + 128)
                placed[side, :, lanes] = pltpu.roll(found[:, lanes], side * SPAN, 1)

        small = skip + count <= NREC

        @pl.when(small)
        def _():
            product(NREC)

        @pl.when(jnp.logical_not(small))
        def _():
            product(NREC + 256)

        @pl.when(side == SIDE - 1)
        def _():
            join(shot // SIDE)

        return shot + 1, begin + count

    def block(i, carry):
        rows_copy(i).wait()
        at = pl.ds(pl.multiple_of(i * DFT_ROWS, DFT_ROWS), DFT_ROWS)
        spectra[at, :] = jnp.dot(
            rows_in[at, :], factors[...], preferred_element_type=jnp.float32
        ).astype(jnp.bfloat16)
        have = (i + 1) * DFT_ROWS

        def ready(carry):
            shot, begin = carry
            return (shot < UNIT) & (begin + counts[0, jnp.minimum(shot, UNIT - 1)] <= have)

        return lax.while_loop(ready, place, carry)

    lax.fori_loop(0, DFT_STEPS, block, (jnp.int32(0), jnp.int32(0)))
    for owner in range(FREQ_DEV):
        owner_copy(owner).wait()


def spread(part, traces, counts, starts, positions, rec_slot):
    height = LAYERS * SLAB_SLOTS + (NOTE_ROWS if part == 0 else 0)
    scalars = pl.BlockSpec(memory_space=pltpu.SMEM)
    anywhere = pl.BlockSpec(memory_space=pl.ANY)
    return pl.pallas_call(
        spread_kernel,
        in_specs=[scalars, scalars, scalars, pl.BlockSpec(memory_space=pltpu.VMEM), anywhere, anywhere],
        out_specs=anywhere,
        out_shape=jax.ShapeDtypeStruct((DEVICES, height, 128), jnp.bfloat16),
        scratch_shapes=[
            pltpu.VMEM((ROWS, NT), jnp.bfloat16),
            pltpu.VMEM((NT, VALUES), jnp.bfloat16),
            pltpu.VMEM((ROWS + 768, VALUES), jnp.bfloat16),
            pltpu.VMEM((SIDE, SLOTS, VALUES), jnp.float32),
            pltpu.VMEM((DEVICES, height, 128), jnp.bfloat16),
            pltpu.SemaphoreType.DMA((DFT_STEPS + 1,)),
            pltpu.SemaphoreType.DMA((FREQ_DEV,)),
        ],
        compiler_params=pltpu.CompilerParams(vmem_limit_bytes=LIMIT),
    )(counts, starts, positions, rec_slot.reshape(1, NREC), traces, jnp.asarray(dft_table(part)))


PHASE_ROWS = 128


def phase_kernel(first_bin, positions, out):
    period = NT * RDIV
    unit = 2.0 * math.pi / period
    scale = 1.0 / math.sqrt(SHOTS)
    tile = 16
    ray = lax.broadcasted_iota(jnp.int32, (tile, RAY_PARAM_COUNT), 1) - RAY_PARAM_COUNT // 2

    def turn(k):
        centred = ((k + period // 2) & (period - 1)) - period // 2
        angle = centred.astype(jnp.float32) * unit
        return jnp.cos(angle), jnp.sin(angle)

    def body(t, carry):
        rows = pl.multiple_of(t * tile, tile)
        delay = positions[pl.ds(rows, tile), :] * ray
        step_cos, step_sin = turn(delay)
        c, s = turn(delay * first_bin[0])
        c, s = c * scale, s * scale
        for f in range(FC):
            out[f, pl.ds(rows, tile), :RAY_PARAM_COUNT] = c.astype(jnp.bfloat16)
            out[f, pl.ds(rows, tile), RAY_PARAM_COUNT:] = s.astype(jnp.bfloat16)
            c, s = c * step_cos - s * step_sin, s * step_cos + c * step_sin
        return carry

    lax.fori_loop(0, PHASE_ROWS // tile, body, 0)


def phases(first_bin, positions):
    return pl.pallas_call(
        phase_kernel,
        grid=(SHOTS // PHASE_ROWS,),
        in_specs=[
            pl.BlockSpec(memory_space=pltpu.SMEM),
            pl.BlockSpec((PHASE_ROWS, RAY_PARAM_COUNT), lambda i: (i, 0)),
        ],
        out_specs=pl.BlockSpec((FC, PHASE_ROWS, 2 * RAY_PARAM_COUNT), lambda i: (0, i, 0)),
        out_shape=jax.ShapeDtypeStruct((FC, SHOTS, 2 * RAY_PARAM_COUNT), jnp.bfloat16),
        compiler_params=pltpu.CompilerParams(vmem_limit_bytes=LIMIT),
    )(first_bin, positions)


PART = 16
PARTS = SLAB_SLOTS // PART
WIDE = PART + 8
LANES = 2 * SLAB_SLOTS
TALL = LANES + 8
DEEP = FC + 8
GROUP = 4


def encode_kernel(blocks, table, earlier, out, raw, factors, wide, lattice, encoded, stage, in_sem, table_sem, out_sem):
    def part_copy(p):
        at = pl.ds(pl.multiple_of(p * PART, PART), PART)
        return pltpu.make_async_copy(blocks.at[:, at], raw.at[:, at], in_sem.at[p])

    def table_copy(g):
        at = pl.ds(g * GROUP, GROUP)
        return pltpu.make_async_copy(table.at[at], factors.at[at], table_sem.at[g])

    for p in range(LAYERS * PARTS):
        part_copy(p).start()
    for g in range(FC // GROUP):
        table_copy(g).start()
    if earlier is not None:
        kept = pltpu.make_async_copy(earlier, out.at[:, :FC], out_sem.at[1])
        kept.start()
    flat = wide.reshape(DEVICES * WIDE, 128)

    def turn(p, carry):
        part_copy(p).wait()
        layer, part = p // PARTS, lax.rem(p, PARTS)
        wide[:, :PART] = raw[:, pl.ds(pl.multiple_of(p * PART, PART), PART)].astype(jnp.float32)
        for s in range(PART):
            turned = jnp.transpose(flat[pl.ds(s, DEVICES, stride=WIDE), :])
            for side in range(SIDE):
                for c in range(2):
                    at = side * SPAN + c * FC
                    lattice[
                        layer * SIDE + side, pl.ds(c * SLAB_SLOTS + part * PART + s, FC, stride=TALL), :
                    ] = turned[at : at + FC, :]
        return carry

    lax.fori_loop(0, LAYERS * PARTS, turn, 0)

    def sum_shots(g, carry):
        table_copy(g).wait()
        for k in range(GROUP):
            f = g * GROUP + k
            at = pl.multiple_of(f * TALL, 8)
            rows = jnp.concatenate(
                [lattice[o, pl.ds(at, LANES), :].astype(jnp.bfloat16) for o in range(UNIT)], axis=1
            )
            both = jnp.dot(rows, factors[f], preferred_element_type=jnp.float32)
            re, im = both[:SLAB_SLOTS], both[SLAB_SLOTS:]
            n = RAY_PARAM_COUNT
            encoded[0, pl.ds(f, SLAB_SLOTS, stride=DEEP), :] = re[:, :n] + im[:, n:]
            encoded[1, pl.ds(f, SLAB_SLOTS, stride=DEEP), :] = im[:, :n] - re[:, n:]
        return carry

    lax.fori_loop(0, FC // GROUP, sum_shots, 0)
    for h in range(2):
        stage[:, :, h * RAY_PARAM_COUNT : (h + 1) * RAY_PARAM_COUNT] = (
            encoded[h].reshape(SLAB_SLOTS, DEEP, RAY_PARAM_COUNT)[:, :FC].astype(jnp.bfloat16)
        )
    target = out if earlier is None else out.at[:, FC:]
    last = pltpu.make_async_copy(stage, target, out_sem.at[0])
    last.start()
    if earlier is not None:
        kept.wait()
    last.wait()


def encode(blocks, table, earlier=None):
    anywhere = pl.BlockSpec(memory_space=pl.ANY)

    def kernel(*refs):
        if earlier is None:
            refs = (*refs[:2], None, *refs[2:])
        encode_kernel(*refs)

    operands = (blocks, table) if earlier is None else (blocks, table, earlier)
    height = FC if earlier is None else FB
    return pl.pallas_call(
        kernel,
        in_specs=[anywhere] * len(operands),
        out_specs=anywhere,
        out_shape=jax.ShapeDtypeStruct((SLAB_SLOTS, height, 2 * RAY_PARAM_COUNT), jnp.bfloat16),
        scratch_shapes=[
            pltpu.VMEM((DEVICES, LAYERS * SLAB_SLOTS, 128), jnp.bfloat16),
            pltpu.VMEM((FC, SHOTS, 2 * RAY_PARAM_COUNT), jnp.bfloat16),
            pltpu.VMEM((DEVICES, WIDE, 128), jnp.float32),
            pltpu.VMEM((UNIT, FC * TALL, 128), jnp.float32),
            pltpu.VMEM((2, SLAB_SLOTS * DEEP, RAY_PARAM_COUNT), jnp.float32),
            pltpu.VMEM((SLAB_SLOTS, FC, 2 * RAY_PARAM_COUNT), jnp.bfloat16),
            pltpu.SemaphoreType.DMA((LAYERS * PARTS,)),
            pltpu.SemaphoreType.DMA((FC // GROUP,)),
            pltpu.SemaphoreType.DMA((2,)),
        ],
        compiler_params=pltpu.CompilerParams(vmem_limit_bytes=LIMIT),
    )(*operands)


def on_device(traces, trace_counts, aperture_start, shot_position, rec_slot):
    own = (trace_counts, aperture_start, shot_position, rec_slot)
    everyone = ("freq", "slab")
    first = lax.all_to_all(spread(0, traces, *own), everyone, split_axis=0, concat_axis=0, tiled=True)
    second = lax.all_to_all(spread(1, traces, *own), everyone, split_axis=0, concat_axis=0, tiled=True)
    note = first[:, LAYERS * SLAB_SLOTS, : 2 * UNIT].astype(jnp.int32)
    positions = (note[:, :UNIT] * 64 + note[:, UNIT:]).T.reshape(LAYERS, SIDE, DEVICES)
    turn = lax.rem(SIDE - lax.rem(lax.axis_index("freq"), SIDE), SIDE)
    positions = lax.dynamic_slice_in_dim(jnp.concatenate([positions, positions], axis=1), turn, SIDE, axis=1)
    positions = jnp.broadcast_to(positions.reshape(SHOTS, 1), (SHOTS, RAY_PARAM_COUNT))
    first_bin = (F0 + lax.axis_index("freq") * FB).astype(jnp.int32).reshape(1)
    low = encode(first, phases(first_bin, positions))
    return encode(second, phases(first_bin + FC, positions), low)


def solution(mesh):
    return jax.shard_map(
        on_device,
        mesh=mesh,
        in_specs=(
            P(("freq", "slab"), None),
            P(("freq", "slab"), None),
            P(("freq", "slab")),
            P(("freq", "slab")),
            P(),
        ),
        out_specs=P("slab", "freq", None),
        check_vma=False,
    )
```

time: 136 us -> 129 us (0.949)
  Pallas kernels: 73.2 us -> 67.3 us
  waiting for transfers between devices: 40.4 us -> 42.9 us
  other arithmetic: 2.09 us -> 0.17 us
    pallas_call x4, Pallas kernels: 60.7 us -> 47.7 us  [the longest x2 27.7 us: spread(): pl.pallas_call(spread_kernel, in_specs=[scalars, scalars, scalars, pl.Blo...]
    pallas_call x1 -> x2, Pallas kernels: 12.5 us -> 19.6 us  [phases(): pl.pallas_call(phase_kernel, grid=(SHOTS // PHASE_ROWS,), in_specs=[pl.Bl...]
    all_to_all x1, waiting for transfers between devices: 27 us -> 29.9 us  [on_device(): lax.all_to_all(spread(0, traces, *own), everyone, split_axis=0, concat_ax...]
    concatenate x1, other arithmetic: 1.96 us -> 0.03 us  [on_device(): jnp.concatenate([positions, positions], axis=1)]
  transfers between devices with their start and end apart: 2 -> 2, of which waited for: 2 -> 2; matrix products, arithmetic and copies ran while one was open for 1% -> 1% of each run, Pallas kernels for 32% -> 31%
where the time goes in v3:
time: 129 us
  Pallas kernels  67.3 us (52%)
  waiting for transfers between devices  42.9 us (33%)
  starting transfers between devices  17.1 us (13%)
    all_to_all x1, waiting for transfers between devices, on_device(): lax.all_to_all(spread(0, traces, *own), everyone, split_axis=0, concat_ax...  29.9 us
    pallas_call x2, Pallas kernels, spread(): pl.pallas_call(spread_kernel, in_specs=[scalars, scalars, scalars, pl.Blo...  27.7 us
    pallas_call x2, Pallas kernels, encode(): pl.pallas_call(kernel, in_specs=[anywhere] * len(operands), out_specs=any...  20.1 us
    pallas_call x2, Pallas kernels, phases(): pl.pallas_call(phase_kernel, grid=(SHOTS // PHASE_ROWS,), in_specs=[pl.Bl...  19.6 us
    all_to_all x1, waiting for transfers between devices, on_device(): lax.all_to_all(spread(1, traces, *own), everyone, split_axis=0, concat_ax...  13 us
    all_to_all x1, starting transfers between devices, on_device(): lax.all_to_all(spread(0, traces, *own), everyone, split_axis=0, concat_ax...  11.4 us
    all_to_all x1, starting transfers between devices, on_device(): lax.all_to_all(spread(1, traces, *own), everyone, split_axis=0, concat_ax...  5.7 us
  transfers between devices with their start and end apart: 2, of which 2 were waited for; matrix products, arithmetic and copies ran while one was open for 1% of the time, Pallas kernels for 31%

profile of v3, /device:TPU:1, one launch (start us, length us, event | category | flops | bytes accessed | tf_op | source)
XLA Modules:
  0.0 128.5 jit_solution(14046900231454210121)
XLA Ops:
  0.0 13.9 %shard_map.74 = bf16[128,104,128]{2,1,0:T(8,128)(2,1)} custom-call(s32[1,8]{1,0:T(1,128)} %counts.3, s32[8]{0:T(128)} %starts.3, s32[8]{0:T(128)} %positions.3, s32[1,512]{1,0:T(1,128)} %bitcast.10, bf16[3072,2048]{1,0:T(8,128)(2,1)} %traces.3, bf16[2048,256]{1,0:T(8,128)(2,1)} %constant.27.clone.table), custom_call_target="tpu_custom_call" | custom-call | tf_op jit(solution)/shard_map/pallas_call | solution.py:154
  13.9 11.4 %all-to-all-start.1 = ((bf16[128,104,128]{2,1,0:T(8,128)(2,1)}), bf16[128,104,128]{2,1,0:T(8,128)(2,1)S(1)}, u32[]{:S(2)}, u32[]{:S(2)}) async-start(bf16[128,104,128]{2,1,0:T(8,128)(2,1)} %shard_map.74), calls=%async_computation.1 | async-start | bytes 6815744 | tf_op jit(solution)/shard_map/all_to_all | solution.py:320
  25.2 13.8 %shard_map.73 = bf16[128,96,128]{2,1,0:T(8,128)(2,1)} custom-call(s32[1,8]{1,0:T(1,128)} %counts.3, s32[8]{0:T(128)} %starts.3, s32[8]{0:T(128)} %positions.3, s32[1,512]{1,0:T(1,128)} %bitcast.11, bf16[3072,2048]{1,0:T(8,128)(2,1)} %traces.3, bf16[2048,256]{1,0:T(8,128)(2,1)} %constant.28.clone.table), custom_call_target="tpu_custom_call" | custom-call | tf_op jit(solution)/shard_map/pallas_call | solution.py:154
  39.1 29.9 %all-to-all-done.1.refs_0_ = bf16[128,104,128]{2,1,0:T(8,128)(2,1)S(1)} async-done(((bf16[128,104,128]{2,1,0:T(8,128)(2,1)}), bf16[128,104,128]{2,1,0:T(8,128)(2,1)S(1)}, u32[]{:S(2)}, u32[]{:S(2)}) %all-to-all-start.1) | async-done | bytes 3407904 | tf_op jit(solution)/shard_map/all_to_all | solution.py:320
  69.0 0.0 copy-start
  69.0 5.7 %all-to-all-start = ((bf16[128,96,128]{2,1,0:T(8,128)(2,1)}), bf16[128,96,128]{2,1,0:T(8,128)(2,1)}, u32[]{:S(2)}, u32[]{:S(2)}) async-start(bf16[128,96,128]{2,1,0:T(8,128)(2,1)} %shard_map.73), calls=%async_computation | async-start | bytes 6291456 | tf_op jit(solution)/shard_map/all_to_all | solution.py:321
  74.7 0.1 slice_convert_fusion
  74.8 0.1 fusion
  74.9 1.0 broadcast_in_dim.8.positions
  75.9 0.0 copy-done
  75.9 9.8 %shard_map.76.refs_1_ = bf16[16,1024,256]{2,1,0:T(8,128)(2,1)} custom-call(s32[1]{0:T(128)} %bitcast.1.first_bin, s32[1024,128]{1,0:T(8,128)} %broadcast_in_dim.8.positions), custom_call_target="tpu_custom_call" | custom-call | tf_op jit(solution)/shard_map/pallas_call | solution.py:203
  85.7 9.8 %shard_map.75.refs_1_ = bf16[16,1024,256]{2,1,0:T(8,128)(2,1)} custom-call(s32[1]{0:T(128)S(6)} %add.13.first_bin, s32[1024,128]{1,0:T(8,128)} %broadcast_in_dim.8.positions), custom_call_target="tpu_custom_call" | custom-call | tf_op jit(solution)/shard_map/pallas_call | solution.py:203
  95.5 6.9 %shard_map.77.refs_2_ = bf16[48,16,256]{2,1,0:T(8,128)(2,1)} custom-call(bf16[128,104,128]{2,1,0:T(8,128)(2,1)} %copy-done, bf16[16,1024,256]{2,1,0:T(8,128)(2,1)} %shard_map.76.refs_1_), custom_call_target="tpu_custom_call" | custom-call | tf_op jit(solution)/shard_map/pallas_call | solution.py:297
  102.4 13.0 %all-to-all-done.refs_0_ = bf16[128,96,128]{2,1,0:T(8,128)(2,1)} async-done(((bf16[128,96,128]{2,1,0:T(8,128)(2,1)}), bf16[128,96,128]{2,1,0:T(8,128)(2,1)}, u32[]{:S(2)}, u32[]{:S(2)}) %all-to-all-start) | async-done | bytes 3145760 | tf_op jit(solution)/shard_map/all_to_all | solution.py:321
  115.4 13.1 %shard_map.78 = bf16[48,32,256]{2,1,0:T(8,128)(2,1)} custom-call(bf16[128,96,128]{2,1,0:T(8,128)(2,1)} %all-to-all-done.refs_0_, bf16[16,1024,256]{2,1,0:T(8,128)(2,1)} %shard_map.75.refs_1_, bf16[48,16,256]{2,1,0:T(8,128)(2,1)} %shard_map.77.refs_2_), custom_call_target="tpu_custom_call" | custom-call | tf_op jit(solution)/shard_map/pallas_call | solution.py:297
  (2 shorter events, 0.1 us)
Async XLA Ops:
  13.9 55.1 %all-to-all-start.1 = ((bf16[128,104,128]{2,1,0:T(8,128)(2,1)}), bf16[128,104,128]{2,1,0:T(8,128)(2,1)S(1)}, u32[]{:S(2)}, u32[]{:S(2)}) async-start(bf16[128,104,128]{2,1,0:T(8,128)(2,1)} %shard_map.74), calls=%async_computation.1 | async-start | bytes 6815744 | tf_op jit(solution)/shard_map/all_to_all | solution.py:320
  69.0 7.0 %copy-start = (bf16[128,104,128]{2,1,0:T(8,128)(2,1)}, bf16[128,104,128]{2,1,0:T(8,128)(2,1)S(1)}, u32[]{:S(2)}) copy-start(bf16[128,104,128]{2,1,0:T(8,128)(2,1)S(1)} %all-to-all-done.1.refs_0_) | copy-start | bytes 10223620
  69.0 46.4 %all-to-all-start = ((bf16[128,96,128]{2,1,0:T(8,128)(2,1)}), bf16[128,96,128]{2,1,0:T(8,128)(2,1)}, u32[]{:S(2)}, u32[]{:S(2)}) async-start(bf16[128,96,128]{2,1,0:T(8,128)(2,1)} %shard_map.73), calls=%async_computation | async-start | bytes 6291456 | tf_op jit(solution)/shard_map/all_to_all | solution.py:321

commit v4 on v3

--- a/solution.py
+++ b/solution.py
@@ -32,7 +32,9 @@
 NOTE_ROWS = 8
 SHOTS = UNIT * DEVICES
 DFT_ROWS = 512
+WINDOW = NREC + 256
 DFT_STEPS = ROWS // DFT_ROWS
+AHEAD = 3
 LIMIT = 60 * 2**20
 
 
@@ -46,7 +48,7 @@
     return table.astype(np.float32).astype(ml_dtypes.bfloat16)
 
 
-def spread_kernel(counts, starts, positions, rec_slot, traces, table, out, rows_in, factors, spectra, placed, stage, in_sem, out_sem):
+def spread_kernel(counts, starts, positions, rec_slot, traces, table, out, rows_in, factors, names, spectra, placed, stage, in_sem, out_sem):
     def rows_copy(i):
         at = pl.ds(pl.multiple_of(i * DFT_ROWS, DFT_ROWS), DFT_ROWS)
         return pltpu.make_async_copy(traces.at[at], rows_in.at[at], in_sem.at[i])
@@ -57,7 +59,7 @@
 
     table_copy = pltpu.make_async_copy(table, factors, in_sem.at[DFT_STEPS])
     table_copy.start()
-    for i in range(DFT_STEPS):
+    for i in range(AHEAD):
         rows_copy(i).start()
     spectra[...] = jnp.zeros(spectra.shape, jnp.bfloat16)
     if stage.shape[1] > LAYERS * SLAB_SLOTS:
@@ -69,6 +71,15 @@
             note = jnp.where(lane == UNIT + k, lax.rem(x, 64), note)
         note = note.astype(jnp.float32).astype(jnp.bfloat16)
         stage[:, LAYERS * SLAB_SLOTS :] = jnp.broadcast_to(note, (DEVICES, NOTE_ROWS, 128))
+    begin = jnp.int32(0)
+    lane = lax.broadcasted_iota(jnp.int32, (1, WINDOW), 1)
+    for k in range(UNIT):
+        skip = lax.rem(begin, 16)
+        shift = lax.rem(skip - starts[k] + NREC, NREC)
+        slots = pltpu.roll(jnp.broadcast_to(rec_slot[...], (8, NREC)), shift, 1)[:1]
+        slots = jnp.concatenate([slots, slots[:, : WINDOW - NREC]], axis=1)
+        names[k : k + 1, :] = jnp.where((lane >= skip) & (lane < skip + counts[0, k]), slots, -1)
+        begin = begin + counts[0, k]
     table_copy.wait()
     group = lax.broadcasted_iota(jnp.int32, (SLOTS, 128), 1) // SPAN
 
@@ -95,14 +106,10 @@
         count = counts[0, shot]
         base = pl.multiple_of((begin // 16) * 16, 16)
         skip = begin - base
-        shift = lax.rem(skip - starts[shot] + NREC, NREC)
-        slots = pltpu.roll(jnp.broadcast_to(rec_slot[...], (8, NREC)), shift, 1)[:1]
 
         def product(depth):
-            names = slots if depth == NREC else jnp.concatenate([slots, slots[:, : depth - NREC]], axis=1)
-            lane = lax.broadcasted_iota(jnp.int32, (1, depth), 1) - skip
-            names = jnp.where((lane >= 0) & (lane < count), names, -1)
-            onehot = (lax.broadcasted_iota(jnp.int32, (SLOTS, depth), 0) == names).astype(jnp.float32)
+            name = names[pl.ds(shot, 1), :depth]
+            onehot = (lax.broadcasted_iota(jnp.int32, (SLOTS, depth), 0) == name).astype(jnp.float32)
             found = jnp.dot(
                 onehot.astype(jnp.bfloat16),
                 spectra[pl.ds(base, depth), :],
@@ -120,7 +127,7 @@
 
         @pl.when(jnp.logical_not(small))
         def _():
-            product(NREC + 256)
+            product(WINDOW)
 
         @pl.when(side == SIDE - 1)
         def _():
@@ -130,6 +137,11 @@
 
     def block(i, carry):
         rows_copy(i).wait()
+
+        @pl.when(i + AHEAD < DFT_STEPS)
+        def _():
+            rows_copy(i + AHEAD).start()
+
         at = pl.ds(pl.multiple_of(i * DFT_ROWS, DFT_ROWS), DFT_ROWS)
         spectra[at, :] = jnp.dot(
             rows_in[at, :], factors[...], preferred_element_type=jnp.float32
@@ -159,7 +171,8 @@
         scratch_shapes=[
             pltpu.VMEM((ROWS, NT), jnp.bfloat16),
             pltpu.VMEM((NT, VALUES), jnp.bfloat16),
-            pltpu.VMEM((ROWS + 768, VALUES), jnp.bfloat16),
+            pltpu.VMEM((UNIT, WINDOW), jnp.int32),
+            pltpu.VMEM((ROWS + WINDOW, VALUES), jnp.bfloat16),
             pltpu.VMEM((SIDE, SLOTS, VALUES), jnp.float32),
             pltpu.VMEM((DEVICES, height, 128), jnp.bfloat16),
             pltpu.SemaphoreType.DMA((DFT_STEPS + 1,)),
@@ -236,7 +249,7 @@
     for g in range(FC // GROUP):
         table_copy(g).start()
     if earlier is not None:
-        kept = pltpu.make_async_copy(earlier, out.at[:, :FC], out_sem.at[1])
+        kept = pltpu.make_async_copy(earlier, stage.at[:, :FC], out_sem.at[1])
         kept.start()
     flat = wide.reshape(DEVICES * WIDE, 128)
 
@@ -272,15 +285,15 @@
         return carry
 
     lax.fori_loop(0, FC // GROUP, sum_shots, 0)
+    own = slice(0, FC) if earlier is None else slice(FC, FB)
     for h in range(2):
-        stage[:, :, h * RAY_PARAM_COUNT : (h + 1) * RAY_PARAM_COUNT] = (
+        stage[:, own, h * RAY_PARAM_COUNT : (h + 1) * RAY_PARAM_COUNT] = (
             encoded[h].reshape(SLAB_SLOTS, DEEP, RAY_PARAM_COUNT)[:, :FC].astype(jnp.bfloat16)
         )
-    target = out if earlier is None else out.at[:, FC:]
-    last = pltpu.make_async_copy(stage, target, out_sem.at[0])
-    last.start()
     if earlier is not None:
         kept.wait()
+    last = pltpu.make_async_copy(stage, out, out_sem.at[0])
+    last.start()
     last.wait()
 
 
@@ -305,7 +318,7 @@
             pltpu.VMEM((DEVICES, WIDE, 128), jnp.float32),
             pltpu.VMEM((UNIT, FC * TALL, 128), jnp.float32),
             pltpu.VMEM((2, SLAB_SLOTS * DEEP, RAY_PARAM_COUNT), jnp.float32),
-            pltpu.VMEM((SLAB_SLOTS, FC, 2 * RAY_PARAM_COUNT), jnp.bfloat16),
+            pltpu.VMEM((SLAB_SLOTS, height, 2 * RAY_PARAM_COUNT), jnp.bfloat16),
             pltpu.SemaphoreType.DMA((LAYERS * PARTS,)),
             pltpu.SemaphoreType.DMA((FC // GROUP,)),
             pltpu.SemaphoreType.DMA((2,)),

time: 129 us -> 123 us (0.953)
  Pallas kernels: 67.3 us -> 59.7 us
    pallas_call x2, Pallas kernels: 20.1 us -> 14 us  [encode(): pl.pallas_call(kernel, in_specs=[anywhere] * len(operands), out_specs=any...]
    pallas_call x2, Pallas kernels: 27.7 us -> 26.2 us  [spread(): pl.pallas_call(spread_kernel, in_specs=[scalars, scalars, scalars, pl.Blo...]
  transfers between devices with their start and end apart: 2 -> 2, of which waited for: 2 -> 2; matrix products, arithmetic and copies ran while one was open for 1% -> 1% of each run, Pallas kernels for 31% -> 32%
where the time goes in v4:
time: 123 us; the launch traced here: 122 us
  Pallas kernels  59.7 us (49%)
  waiting for transfers between devices  43.6 us (35%)
  starting transfers between devices  17.5 us (14%)
    all_to_all x1, waiting for transfers between devices, on_device(): lax.all_to_all(spread(0, traces, *own), everyone, split_axis=0, concat_ax...  30.6 us
    pallas_call x2, Pallas kernels, spread(): pl.pallas_call(spread_kernel, in_specs=[scalars, scalars, scalars, pl.Blo...  26.2 us
    pallas_call x2, Pallas kernels, phases(): pl.pallas_call(phase_kernel, grid=(SHOTS // PHASE_ROWS,), in_specs=[pl.Bl...  19.6 us
    pallas_call x2, Pallas kernels, encode(): pl.pallas_call(kernel, in_specs=[anywhere] * len(operands), out_specs=any...  14 us
    all_to_all x1, waiting for transfers between devices, on_device(): lax.all_to_all(spread(1, traces, *own), everyone, split_axis=0, concat_ax...  13 us
    all_to_all x1, starting transfers between devices, on_device(): lax.all_to_all(spread(0, traces, *own), everyone, split_axis=0, concat_ax...  11.8 us
    all_to_all x1, starting transfers between devices, on_device(): lax.all_to_all(spread(1, traces, *own), everyone, split_axis=0, concat_ax...  5.7 us
  transfers between devices with their start and end apart: 2, of which 2 were waited for; matrix products, arithmetic and copies ran while one was open for 1% of the time, Pallas kernels for 32%

profile of v4, /device:TPU:1, one launch (start us, length us, event | category | flops | bytes accessed | tf_op | source)
XLA Modules:
  0.0 122.1 jit_solution(2194235179768062868)
XLA Ops:
  0.0 13.1 %shard_map.74 = bf16[128,104,128]{2,1,0:T(8,128)(2,1)} custom-call(s32[1,8]{1,0:T(1,128)} %counts.3, s32[8]{0:T(128)} %starts.3, s32[8]{0:T(128)} %positions.3, s32[1,512]{1,0:T(1,128)} %bitcast.10, bf16[3072,2048]{1,0:T(8,128)(2,1)} %traces.3, bf16[2048,256]{1,0:T(8,128)(2,1)} %constant.27.clone.table), custom_call_target="tpu_custom_call" | custom-call | tf_op jit(solution)/shard_map/pallas_call | solution.py:166
  13.1 11.8 %all-to-all-start.1 = ((bf16[128,104,128]{2,1,0:T(8,128)(2,1)}), bf16[128,104,128]{2,1,0:T(8,128)(2,1)S(1)}, u32[]{:S(2)}, u32[]{:S(2)}) async-start(bf16[128,104,128]{2,1,0:T(8,128)(2,1)} %shard_map.74), calls=%async_computation.1 | async-start | bytes 6815744 | tf_op jit(solution)/shard_map/all_to_all | solution.py:333
  25.0 13.1 %shard_map.73 = bf16[128,96,128]{2,1,0:T(8,128)(2,1)} custom-call(s32[1,8]{1,0:T(1,128)} %counts.3, s32[8]{0:T(128)} %starts.3, s32[8]{0:T(128)} %positions.3, s32[1,512]{1,0:T(1,128)} %bitcast.11, bf16[3072,2048]{1,0:T(8,128)(2,1)} %traces.3, bf16[2048,256]{1,0:T(8,128)(2,1)} %constant.28.clone.table), custom_call_target="tpu_custom_call" | custom-call | tf_op jit(solution)/shard_map/pallas_call | solution.py:166
  38.0 30.6 %all-to-all-done.1.refs_0_ = bf16[128,104,128]{2,1,0:T(8,128)(2,1)S(1)} async-done(((bf16[128,104,128]{2,1,0:T(8,128)(2,1)}), bf16[128,104,128]{2,1,0:T(8,128)(2,1)S(1)}, u32[]{:S(2)}, u32[]{:S(2)}) %all-to-all-start.1) | async-done | bytes 3407904 | tf_op jit(solution)/shard_map/all_to_all | solution.py:333
  68.7 0.0 copy-start
  68.7 5.7 %all-to-all-start = ((bf16[128,96,128]{2,1,0:T(8,128)(2,1)}), bf16[128,96,128]{2,1,0:T(8,128)(2,1)}, u32[]{:S(2)}, u32[]{:S(2)}) async-start(bf16[128,96,128]{2,1,0:T(8,128)(2,1)} %shard_map.73), calls=%async_computation | async-start | bytes 6291456 | tf_op jit(solution)/shard_map/all_to_all | solution.py:334
  74.4 0.1 slice_convert_fusion
  74.5 0.1 fusion
  74.6 1.0 broadcast_in_dim.8.positions
  75.6 0.0 copy-done
  75.6 9.8 %shard_map.76.refs_1_ = bf16[16,1024,256]{2,1,0:T(8,128)(2,1)} custom-call(s32[1]{0:T(128)} %bitcast.1.first_bin, s32[1024,128]{1,0:T(8,128)} %broadcast_in_dim.8.positions), custom_call_target="tpu_custom_call" | custom-call | tf_op jit(solution)/shard_map/pallas_call | solution.py:216
  85.4 9.8 %shard_map.75.refs_1_ = bf16[16,1024,256]{2,1,0:T(8,128)(2,1)} custom-call(s32[1]{0:T(128)S(6)} %add.13.first_bin, s32[1024,128]{1,0:T(8,128)} %broadcast_in_dim.8.positions), custom_call_target="tpu_custom_call" | custom-call | tf_op jit(solution)/shard_map/pallas_call | solution.py:216
  95.2 6.9 %shard_map.77.refs_2_ = bf16[48,16,256]{2,1,0:T(8,128)(2,1)} custom-call(bf16[128,104,128]{2,1,0:T(8,128)(2,1)} %copy-done, bf16[16,1024,256]{2,1,0:T(8,128)(2,1)} %shard_map.76.refs_1_), custom_call_target="tpu_custom_call" | custom-call | tf_op jit(solution)/shard_map/pallas_call | solution.py:310
  102.1 13.0 %all-to-all-done.refs_0_ = bf16[128,96,128]{2,1,0:T(8,128)(2,1)} async-done(((bf16[128,96,128]{2,1,0:T(8,128)(2,1)}), bf16[128,96,128]{2,1,0:T(8,128)(2,1)}, u32[]{:S(2)}, u32[]{:S(2)}) %all-to-all-start) | async-done | bytes 3145760 | tf_op jit(solution)/shard_map/all_to_all | solution.py:334
  115.1 7.0 %shard_map.78 = bf16[48,32,256]{2,1,0:T(8,128)(2,1)} custom-call(bf16[128,96,128]{2,1,0:T(8,128)(2,1)} %all-to-all-done.refs_0_, bf16[16,1024,256]{2,1,0:T(8,128)(2,1)} %shard_map.75.refs_1_, bf16[48,16,256]{2,1,0:T(8,128)(2,1)} %shard_map.77.refs_2_), custom_call_target="tpu_custom_call" | custom-call | tf_op jit(solution)/shard_map/pallas_call | solution.py:310
  (2 shorter events, 0.1 us)
Async XLA Ops:
  13.1 55.6 %all-to-all-start.1 = ((bf16[128,104,128]{2,1,0:T(8,128)(2,1)}), bf16[128,104,128]{2,1,0:T(8,128)(2,1)S(1)}, u32[]{:S(2)}, u32[]{:S(2)}) async-start(bf16[128,104,128]{2,1,0:T(8,128)(2,1)} %shard_map.74), calls=%async_computation.1 | async-start | bytes 6815744 | tf_op jit(solution)/shard_map/all_to_all | solution.py:333
  68.7 7.0 %copy-start = (bf16[128,104,128]{2,1,0:T(8,128)(2,1)}, bf16[128,104,128]{2,1,0:T(8,128)(2,1)S(1)}, u32[]{:S(2)}) copy-start(bf16[128,104,128]{2,1,0:T(8,128)(2,1)S(1)} %all-to-all-done.1.refs_0_) | copy-start | bytes 10223620
  68.7 46.4 %all-to-all-start = ((bf16[128,96,128]{2,1,0:T(8,128)(2,1)}), bf16[128,96,128]{2,1,0:T(8,128)(2,1)}, u32[]{:S(2)}, u32[]{:S(2)}) async-start(bf16[128,96,128]{2,1,0:T(8,128)(2,1)} %shard_map.73), calls=%async_computation | async-start | bytes 6291456 | tf_op jit(solution)/shard_map/all_to_all | solution.py:334

commit v5 on v4

--- a/solution.py
+++ b/solution.py
@@ -29,7 +29,8 @@
 SPAN = 2 * FC
 SIDE = 128 // SPAN
 LAYERS = UNIT // SIDE
-NOTE_ROWS = 8
+PAIRS = LAYERS * SLAB_SLOTS // 2
+NOTE_ROWS = 2
 SHOTS = UNIT * DEVICES
 DFT_ROWS = 512
 WINDOW = NREC + 256
@@ -49,6 +50,8 @@
 
 
 def spread_kernel(counts, starts, positions, rec_slot, traces, table, out, rows_in, factors, names, spectra, placed, stage, in_sem, out_sem):
+    noted = len(stage.shape) == 4
+
     def rows_copy(i):
         at = pl.ds(pl.multiple_of(i * DFT_ROWS, DFT_ROWS), DFT_ROWS)
         return pltpu.make_async_copy(traces.at[at], rows_in.at[at], in_sem.at[i])
@@ -62,15 +65,15 @@
     for i in range(AHEAD):
         rows_copy(i).start()
     spectra[...] = jnp.zeros(spectra.shape, jnp.bfloat16)
-    if stage.shape[1] > LAYERS * SLAB_SLOTS:
-        lane = lax.broadcasted_iota(jnp.int32, (1, NOTE_ROWS, 128), 2)
-        note = jnp.zeros((1, NOTE_ROWS, 128), jnp.int32)
+    if noted:
+        lane = lax.broadcasted_iota(jnp.int32, (1, 1, NOTE_ROWS, 128), 3)
+        note = jnp.zeros((1, 1, NOTE_ROWS, 128), jnp.int32)
         for k in range(UNIT):
             x = positions[k]
             note = jnp.where(lane == k, x // 64, note)
             note = jnp.where(lane == UNIT + k, lax.rem(x, 64), note)
         note = note.astype(jnp.float32).astype(jnp.bfloat16)
-        stage[:, LAYERS * SLAB_SLOTS :] = jnp.broadcast_to(note, (DEVICES, NOTE_ROWS, 128))
+        stage[:, PAIRS:] = jnp.broadcast_to(note, (DEVICES, 1, NOTE_ROWS, 128))
     begin = jnp.int32(0)
     lane = lax.broadcasted_iota(jnp.int32, (1, WINDOW), 1)
     for k in range(UNIT):
@@ -84,7 +87,8 @@
     group = lax.broadcasted_iota(jnp.int32, (SLOTS, 128), 1) // SPAN
 
     def join(layer):
-        at = pl.ds(pl.multiple_of(layer * SLAB_SLOTS, 16), SLAB_SLOTS)
+        height = (SLAB_SLOTS // 2, 2) if noted else (SLAB_SLOTS,)
+        at = pl.ds(layer * height[0] if noted else pl.multiple_of(layer * SLAB_SLOTS, 16), height[0])
         for tile in range(VALUES // 128):
             pieces = [placed[side, :, tile * 128 : tile * 128 + 128] for side in range(SIDE)]
             for k in range(SIDE):
@@ -93,7 +97,7 @@
                     joined = jnp.where(group == g, pieces[(g - k) % SIDE], joined)
                 owner = tile * SIDE + k
                 stage[owner * SLAB_DEV : (owner + 1) * SLAB_DEV, at] = joined.astype(jnp.bfloat16).reshape(
-                    SLAB_DEV, SLAB_SLOTS, 128
+                    SLAB_DEV, *height, 128
                 )
 
                 @pl.when(layer == LAYERS - 1)
@@ -160,21 +164,21 @@
 
 
 def spread(part, traces, counts, starts, positions, rec_slot):
-    height = LAYERS * SLAB_SLOTS + (NOTE_ROWS if part == 0 else 0)
+    rows = (PAIRS + 1, 2) if part == 0 else (LAYERS * SLAB_SLOTS,)
     scalars = pl.BlockSpec(memory_space=pltpu.SMEM)
     anywhere = pl.BlockSpec(memory_space=pl.ANY)
     return pl.pallas_call(
         spread_kernel,
         in_specs=[scalars, scalars, scalars, pl.BlockSpec(memory_space=pltpu.VMEM), anywhere, anywhere],
         out_specs=anywhere,
-        out_shape=jax.ShapeDtypeStruct((DEVICES, height, 128), jnp.bfloat16),
+        out_shape=jax.ShapeDtypeStruct((DEVICES, *rows, 128), jnp.bfloat16),
         scratch_shapes=[
             pltpu.VMEM((ROWS, NT), jnp.bfloat16),
             pltpu.VMEM((NT, VALUES), jnp.bfloat16),
             pltpu.VMEM((UNIT, WINDOW), jnp.int32),
             pltpu.VMEM((ROWS + WINDOW, VALUES), jnp.bfloat16),
             pltpu.VMEM((SIDE, SLOTS, VALUES), jnp.float32),
-            pltpu.VMEM((DEVICES, height, 128), jnp.bfloat16),
+            pltpu.VMEM((DEVICES, *rows, 128), jnp.bfloat16),
             pltpu.SemaphoreType.DMA((DFT_STEPS + 1,)),
             pltpu.SemaphoreType.DMA((FREQ_DEV,)),
         ],
@@ -236,8 +240,13 @@
 
 
 def encode_kernel(blocks, table, earlier, out, raw, factors, wide, lattice, encoded, stage, in_sem, table_sem, out_sem):
+    def part_rows(p):
+        if len(raw.shape) == 4:
+            return pl.ds(p * (PART // 2), PART // 2)
+        return pl.ds(pl.multiple_of(p * PART, PART), PART)
+
     def part_copy(p):
-        at = pl.ds(pl.multiple_of(p * PART, PART), PART)
+        at = part_rows(p)
         return pltpu.make_async_copy(blocks.at[:, at], raw.at[:, at], in_sem.at[p])
 
     def table_copy(g):
@@ -246,8 +255,6 @@
 
     for p in range(LAYERS * PARTS):
         part_copy(p).start()
-    for g in range(FC // GROUP):
-        table_copy(g).start()
     if earlier is not None:
         kept = pltpu.make_async_copy(earlier, stage.at[:, :FC], out_sem.at[1])
         kept.start()
@@ -255,8 +262,14 @@
 
     def turn(p, carry):
         part_copy(p).wait()
+
+        @pl.when(p == 0)
+        def _():
+            for g in range(FC // GROUP):
+                table_copy(g).start()
+
         layer, part = p // PARTS, lax.rem(p, PARTS)
-        wide[:, :PART] = raw[:, pl.ds(pl.multiple_of(p * PART, PART), PART)].astype(jnp.float32)
+        wide[:, :PART] = raw[:, part_rows(p)].reshape(DEVICES, PART, 128).astype(jnp.float32)
         for s in range(PART):
             turned = jnp.transpose(flat[pl.ds(s, DEVICES, stride=WIDE), :])
             for side in range(SIDE):
@@ -307,13 +320,14 @@
 
     operands = (blocks, table) if earlier is None else (blocks, table, earlier)
     height = FC if earlier is None else FB
+    rows = (PAIRS, 2) if blocks.ndim == 4 else (LAYERS * SLAB_SLOTS,)
     return pl.pallas_call(
         kernel,
         in_specs=[anywhere] * len(operands),
         out_specs=anywhere,
         out_shape=jax.ShapeDtypeStruct((SLAB_SLOTS, height, 2 * RAY_PARAM_COUNT), jnp.bfloat16),
         scratch_shapes=[
-            pltpu.VMEM((DEVICES, LAYERS * SLAB_SLOTS, 128), jnp.bfloat16),
+            pltpu.VMEM((DEVICES, *rows, 128), jnp.bfloat16),
             pltpu.VMEM((FC, SHOTS, 2 * RAY_PARAM_COUNT), jnp.bfloat16),
             pltpu.VMEM((DEVICES, WIDE, 128), jnp.float32),
             pltpu.VMEM((UNIT, FC * TALL, 128), jnp.float32),
@@ -332,7 +346,7 @@
     everyone = ("freq", "slab")
     first = lax.all_to_all(spread(0, traces, *own), everyone, split_axis=0, concat_axis=0, tiled=True)
     second = lax.all_to_all(spread(1, traces, *own), everyone, split_axis=0, concat_axis=0, tiled=True)
-    note = first[:, LAYERS * SLAB_SLOTS, : 2 * UNIT].astype(jnp.int32)
+    note = first[:, PAIRS, 0, : 2 * UNIT].astype(jnp.int32)
     positions = (note[:, :UNIT] * 64 + note[:, UNIT:]).T.reshape(LAYERS, SIDE, DEVICES)
     turn = lax.rem(SIDE - lax.rem(lax.axis_index("freq"), SIDE), SIDE)
     positions = lax.dynamic_slice_in_dim(jnp.concatenate([positions, positions], axis=1), turn, SIDE, axis=1)

time: 123 us -> 121 us (0.984)
  waiting for transfers between devices: 43.6 us -> 40.5 us
  Pallas kernels: 59.7 us -> 61.2 us
    all_to_all x1, waiting for transfers between devices: 30.6 us -> 28.3 us  [on_device(): lax.all_to_all(spread(0, traces, *own), everyone, split_axis=0, concat_ax...]
    pallas_call x2, Pallas kernels: 26.2 us -> 27.6 us  [spread(): pl.pallas_call(spread_kernel, in_specs=[scalars, scalars, scalars, pl.Blo...]
  transfers between devices with their start and end apart: 2 -> 2, of which waited for: 2 -> 2; matrix products, arithmetic and copies ran while one was open for 1% -> 1% of each run, Pallas kernels for 32% -> 34%
where the time goes in v5:
time: 121 us; the launch traced here: 120 us
  Pallas kernels  61.2 us (51%)
  waiting for transfers between devices  40.5 us (33%)
  starting transfers between devices  17.2 us (14%)
    all_to_all x1, waiting for transfers between devices, on_device(): lax.all_to_all(spread(0, traces, *own), everyone, split_axis=0, concat_ax...  28.3 us
    pallas_call x2, Pallas kernels, spread(): pl.pallas_call(spread_kernel, in_specs=[scalars, scalars, scalars, pl.Blo...  27.6 us
    pallas_call x2, Pallas kernels, phases(): pl.pallas_call(phase_kernel, grid=(SHOTS // PHASE_ROWS,), in_specs=[pl.Bl...  19.6 us
    pallas_call x2, Pallas kernels, encode(): pl.pallas_call(kernel, in_specs=[anywhere] * len(operands), out_specs=any...  14 us
    all_to_all x1, waiting for transfers between devices, on_device(): lax.all_to_all(spread(1, traces, *own), everyone, split_axis=0, concat_ax...  12.2 us
    all_to_all x1, starting transfers between devices, on_device(): lax.all_to_all(spread(0, traces, *own), everyone, split_axis=0, concat_ax...  11.4 us
    all_to_all x1, starting transfers between devices, on_device(): lax.all_to_all(spread(1, traces, *own), everyone, split_axis=0, concat_ax...  5.75 us
  transfers between devices with their start and end apart: 2, of which 2 were waited for; matrix products, arithmetic and copies ran while one was open for 1% of the time, Pallas kernels for 34%

profile of v5, /device:TPU:1, one launch (start us, length us, event | category | flops | bytes accessed | tf_op | source)
XLA Modules:
  0.0 120.2 jit_solution(245308038811382541)
XLA Ops:
  0.0 14.4 %shard_map.74 = bf16[128,49,2,128]{3,2,1,0:T(2,128)(2,1)} custom-call(s32[1,8]{1,0:T(1,128)} %counts.3, s32[8]{0:T(128)} %starts.3, s32[8]{0:T(128)} %positions.3, s32[1,512]{1,0:T(1,128)} %bitcast.10, bf16[3072,2048]{1,0:T(8,128)(2,1)} %traces.3, bf16[2048,256]{1,0:T(8,128)(2,1)} %constant.27.clone.table), custom_call_target="tpu_custom_call" | custom-call | tf_op jit(solution)/shard_map/pallas_call | solution.py:170
  14.4 11.4 %all-to-all-start.1 = ((bf16[128,49,2,128]{3,2,1,0:T(2,128)(2,1)}), bf16[128,49,2,128]{3,2,1,0:T(2,128)(2,1)S(1)}, u32[]{:S(2)}, u32[]{:S(2)}) async-start(bf16[128,49,2,128]{3,2,1,0:T(2,128)(2,1)} %shard_map.74), calls=%async_computation.1 | async-start | bytes 6422528 | tf_op jit(solution)/shard_map/all_to_all | solution.py:347
  25.8 13.3 %shard_map.73 = bf16[128,96,128]{2,1,0:T(8,128)(2,1)} custom-call(s32[1,8]{1,0:T(1,128)} %counts.3, s32[8]{0:T(128)} %starts.3, s32[8]{0:T(128)} %positions.3, s32[1,512]{1,0:T(1,128)} %bitcast.11, bf16[3072,2048]{1,0:T(8,128)(2,1)} %traces.3, bf16[2048,256]{1,0:T(8,128)(2,1)} %constant.28.clone.table), custom_call_target="tpu_custom_call" | custom-call | tf_op jit(solution)/shard_map/pallas_call | solution.py:170
  39.1 28.3 %all-to-all-done.1.refs_0_ = bf16[128,49,2,128]{3,2,1,0:T(2,128)(2,1)S(1)} async-done(((bf16[128,49,2,128]{3,2,1,0:T(2,128)(2,1)}), bf16[128,49,2,128]{3,2,1,0:T(2,128)(2,1)S(1)}, u32[]{:S(2)}, u32[]{:S(2)}) %all-to-all-start.1) | async-done | bytes 3211296 | tf_op jit(solution)/shard_map/all_to_all | solution.py:347
  67.4 0.0 copy-start
  67.4 5.7 %all-to-all-start = ((bf16[128,96,128]{2,1,0:T(8,128)(2,1)}), bf16[128,96,128]{2,1,0:T(8,128)(2,1)}, u32[]{:S(2)}, u32[]{:S(2)}) async-start(bf16[128,96,128]{2,1,0:T(8,128)(2,1)} %shard_map.73), calls=%async_computation | async-start | bytes 6291456 | tf_op jit(solution)/shard_map/all_to_all | solution.py:348
  73.1 0.1 slice_convert_fusion
  73.2 0.0 copy-done
  73.2 0.1 fusion
  73.4 1.0 broadcast_in_dim.8.positions
  74.4 9.8 %shard_map.76.refs_1_ = bf16[16,1024,256]{2,1,0:T(8,128)(2,1)} custom-call(s32[1]{0:T(128)} %bitcast.1.first_bin, s32[1024,128]{1,0:T(8,128)} %broadcast_in_dim.8.positions), custom_call_target="tpu_custom_call" | custom-call | tf_op jit(solution)/shard_map/pallas_call | solution.py:220
  84.1 9.8 %shard_map.75.refs_1_ = bf16[16,1024,256]{2,1,0:T(8,128)(2,1)} custom-call(s32[1]{0:T(128)S(6)} %add.13.first_bin, s32[1024,128]{1,0:T(8,128)} %broadcast_in_dim.8.positions), custom_call_target="tpu_custom_call" | custom-call | tf_op jit(solution)/shard_map/pallas_call | solution.py:220
  93.9 7.7 %shard_map.77.refs_2_ = bf16[48,16,256]{2,1,0:T(8,128)(2,1)} custom-call(bf16[128,49,2,128]{3,2,1,0:T(2,128)(2,1)} %copy-done, bf16[16,1024,256]{2,1,0:T(8,128)(2,1)} %shard_map.76.refs_1_), custom_call_target="tpu_custom_call" | custom-call | tf_op jit(solution)/shard_map/pallas_call | solution.py:324
  101.6 12.2 %all-to-all-done.refs_0_ = bf16[128,96,128]{2,1,0:T(8,128)(2,1)} async-done(((bf16[128,96,128]{2,1,0:T(8,128)(2,1)}), bf16[128,96,128]{2,1,0:T(8,128)(2,1)}, u32[]{:S(2)}, u32[]{:S(2)}) %all-to-all-start) | async-done | bytes 3145760 | tf_op jit(solution)/shard_map/all_to_all | solution.py:348
  113.8 6.4 %shard_map.78 = bf16[48,32,256]{2,1,0:T(8,128)(2,1)} custom-call(bf16[128,96,128]{2,1,0:T(8,128)(2,1)} %all-to-all-done.refs_0_, bf16[16,1024,256]{2,1,0:T(8,128)(2,1)} %shard_map.75.refs_1_, bf16[48,16,256]{2,1,0:T(8,128)(2,1)} %shard_map.77.refs_2_), custom_call_target="tpu_custom_call" | custom-call | tf_op jit(solution)/shard_map/pallas_call | solution.py:324
  (2 shorter events, 0.1 us)
Async XLA Ops:
  14.4 53.0 %all-to-all-start.1 = ((bf16[128,49,2,128]{3,2,1,0:T(2,128)(2,1)}), bf16[128,49,2,128]{3,2,1,0:T(2,128)(2,1)S(1)}, u32[]{:S(2)}, u32[]{:S(2)}) async-start(bf16[128,49,2,128]{3,2,1,0:T(2,128)(2,1)} %shard_map.74), calls=%async_computation.1 | async-start | bytes 6422528 | tf_op jit(solution)/shard_map/all_to_all | solution.py:347
  67.4 5.8 %copy-start = (bf16[128,49,2,128]{3,2,1,0:T(2,128)(2,1)}, bf16[128,49,2,128]{3,2,1,0:T(2,128)(2,1)S(1)}, u32[]{:S(2)}) copy-start(bf16[128,49,2,128]{3,2,1,0:T(2,128)(2,1)S(1)} %all-to-all-done.1.refs_0_) | copy-start | bytes 9633796
  67.4 46.5 %all-to-all-start = ((bf16[128,96,128]{2,1,0:T(8,128)(2,1)}), bf16[128,96,128]{2,1,0:T(8,128)(2,1)}, u32[]{:S(2)}, u32[]{:S(2)}) async-start(bf16[128,96,128]{2,1,0:T(8,128)(2,1)} %shard_map.73), calls=%async_computation | async-start | bytes 6291456 | tf_op jit(solution)/shard_map/all_to_all | solution.py:348

commit v6 on v5

--- a/solution.py
+++ b/solution.py
@@ -32,10 +32,10 @@
 PAIRS = LAYERS * SLAB_SLOTS // 2
 NOTE_ROWS = 2
 SHOTS = UNIT * DEVICES
-DFT_ROWS = 512
+DFT_ROWS = 768
 WINDOW = NREC + 256
 DFT_STEPS = ROWS // DFT_ROWS
-AHEAD = 3
+AHEAD = 2
 LIMIT = 60 * 2**20
 
 
@@ -271,7 +271,7 @@
         layer, part = p // PARTS, lax.rem(p, PARTS)
         wide[:, :PART] = raw[:, part_rows(p)].reshape(DEVICES, PART, 128).astype(jnp.float32)
         for s in range(PART):
-            turned = jnp.transpose(flat[pl.ds(s, DEVICES, stride=WIDE), :])
+            turned = jnp.transpose(flat[pl.ds(s, DEVICES, stride=WIDE), :].astype(jnp.bfloat16)).astype(jnp.float32)
             for side in range(SIDE):
                 for c in range(2):
                     at = side * SPAN + c * FC

time: 121 us -> 121 us (level)
  no operation moved by 1% of the time
where the time goes in v6:
time: 121 us; the launch traced here: 120 us
  Pallas kernels  60.6 us (50%)
  waiting for transfers between devices  40.7 us (34%)
  starting transfers between devices  17.5 us (14%)
    all_to_all x1, waiting for transfers between devices, on_device(): lax.all_to_all(spread(0, traces, *own), everyone, split_axis=0, concat_ax...  28.5 us
    pallas_call x2, Pallas kernels, spread(): pl.pallas_call(spread_kernel, in_specs=[scalars, scalars, scalars, pl.Blo...  27.1 us
    pallas_call x2, Pallas kernels, phases(): pl.pallas_call(phase_kernel, grid=(SHOTS // PHASE_ROWS,), in_specs=[pl.Bl...  19.6 us
    pallas_call x2, Pallas kernels, encode(): pl.pallas_call(kernel, in_specs=[anywhere] * len(operands), out_specs=any...  14 us
    all_to_all x1, waiting for transfers between devices, on_device(): lax.all_to_all(spread(1, traces, *own), everyone, split_axis=0, concat_ax...  12.2 us
    all_to_all x1, starting transfers between devices, on_device(): lax.all_to_all(spread(0, traces, *own), everyone, split_axis=0, concat_ax...  11.7 us
    all_to_all x1, starting transfers between devices, on_device(): lax.all_to_all(spread(1, traces, *own), everyone, split_axis=0, concat_ax...  5.75 us
  transfers between devices with their start and end apart: 2, of which 2 were waited for; matrix products, arithmetic and copies ran while one was open for 1% of the time, Pallas kernels for 34%

profile of v6, /device:TPU:1, one launch (start us, length us, event | category | flops | bytes accessed | tf_op | source)
XLA Modules:
  0.0 120.1 jit_solution(14799507650326328295)
XLA Ops:
  0.0 14.1 %shard_map.74 = bf16[128,49,2,128]{3,2,1,0:T(2,128)(2,1)} custom-call(s32[1,8]{1,0:T(1,128)} %counts.3, s32[8]{0:T(128)} %starts.3, s32[8]{0:T(128)} %positions.3, s32[1,512]{1,0:T(1,128)} %bitcast.10, bf16[3072,2048]{1,0:T(8,128)(2,1)} %traces.3, bf16[2048,256]{1,0:T(8,128)(2,1)} %constant.27.clone.table), custom_call_target="tpu_custom_call" | custom-call | tf_op jit(solution)/shard_map/pallas_call | solution.py:170
  14.1 11.7 %all-to-all-start.1 = ((bf16[128,49,2,128]{3,2,1,0:T(2,128)(2,1)}), bf16[128,49,2,128]{3,2,1,0:T(2,128)(2,1)S(1)}, u32[]{:S(2)}, u32[]{:S(2)}) async-start(bf16[128,49,2,128]{3,2,1,0:T(2,128)(2,1)} %shard_map.74), calls=%async_computation.1 | async-start | bytes 6422528 | tf_op jit(solution)/shard_map/all_to_all | solution.py:347
  25.8 13.0 %shard_map.73 = bf16[128,96,128]{2,1,0:T(8,128)(2,1)} custom-call(s32[1,8]{1,0:T(1,128)} %counts.3, s32[8]{0:T(128)} %starts.3, s32[8]{0:T(128)} %positions.3, s32[1,512]{1,0:T(1,128)} %bitcast.11, bf16[3072,2048]{1,0:T(8,128)(2,1)} %traces.3, bf16[2048,256]{1,0:T(8,128)(2,1)} %constant.28.clone.table), custom_call_target="tpu_custom_call" | custom-call | tf_op jit(solution)/shard_map/pallas_call | solution.py:170
  38.8 28.5 %all-to-all-done.1.refs_0_ = bf16[128,49,2,128]{3,2,1,0:T(2,128)(2,1)S(1)} async-done(((bf16[128,49,2,128]{3,2,1,0:T(2,128)(2,1)}), bf16[128,49,2,128]{3,2,1,0:T(2,128)(2,1)S(1)}, u32[]{:S(2)}, u32[]{:S(2)}) %all-to-all-start.1) | async-done | bytes 3211296 | tf_op jit(solution)/shard_map/all_to_all | solution.py:347
  67.4 0.0 copy-start
  67.4 5.7 %all-to-all-start = ((bf16[128,96,128]{2,1,0:T(8,128)(2,1)}), bf16[128,96,128]{2,1,0:T(8,128)(2,1)}, u32[]{:S(2)}, u32[]{:S(2)}) async-start(bf16[128,96,128]{2,1,0:T(8,128)(2,1)} %shard_map.73), calls=%async_computation | async-start | bytes 6291456 | tf_op jit(solution)/shard_map/all_to_all | solution.py:348
  73.1 0.1 slice_convert_fusion
  73.2 0.0 copy-done
  73.2 0.1 fusion
  73.4 1.0 broadcast_in_dim.8.positions
  74.4 9.8 %shard_map.76.refs_1_ = bf16[16,1024,256]{2,1,0:T(8,128)(2,1)} custom-call(s32[1]{0:T(128)} %bitcast.1.first_bin, s32[1024,128]{1,0:T(8,128)} %broadcast_in_dim.8.positions), custom_call_target="tpu_custom_call" | custom-call | tf_op jit(solution)/shard_map/pallas_call | solution.py:220
  84.2 9.8 %shard_map.75.refs_1_ = bf16[16,1024,256]{2,1,0:T(8,128)(2,1)} custom-call(s32[1]{0:T(128)S(6)} %add.13.first_bin, s32[1024,128]{1,0:T(8,128)} %broadcast_in_dim.8.positions), custom_call_target="tpu_custom_call" | custom-call | tf_op jit(solution)/shard_map/pallas_call | solution.py:220
  94.0 7.7 %shard_map.77.refs_2_ = bf16[48,16,256]{2,1,0:T(8,128)(2,1)} custom-call(bf16[128,49,2,128]{3,2,1,0:T(2,128)(2,1)} %copy-done, bf16[16,1024,256]{2,1,0:T(8,128)(2,1)} %shard_map.76.refs_1_), custom_call_target="tpu_custom_call" | custom-call | tf_op jit(solution)/shard_map/pallas_call | solution.py:324
  101.7 12.2 %all-to-all-done.refs_0_ = bf16[128,96,128]{2,1,0:T(8,128)(2,1)} async-done(((bf16[128,96,128]{2,1,0:T(8,128)(2,1)}), bf16[128,96,128]{2,1,0:T(8,128)(2,1)}, u32[]{:S(2)}, u32[]{:S(2)}) %all-to-all-start) | async-done | bytes 3145760 | tf_op jit(solution)/shard_map/all_to_all | solution.py:348
  113.8 6.3 %shard_map.78 = bf16[48,32,256]{2,1,0:T(8,128)(2,1)} custom-call(bf16[128,96,128]{2,1,0:T(8,128)(2,1)} %all-to-all-done.refs_0_, bf16[16,1024,256]{2,1,0:T(8,128)(2,1)} %shard_map.75.refs_1_, bf16[48,16,256]{2,1,0:T(8,128)(2,1)} %shard_map.77.refs_2_), custom_call_target="tpu_custom_call" | custom-call | tf_op jit(solution)/shard_map/pallas_call | solution.py:324
  (2 shorter events, 0.1 us)
Async XLA Ops:
  14.1 53.3 %all-to-all-start.1 = ((bf16[128,49,2,128]{3,2,1,0:T(2,128)(2,1)}), bf16[128,49,2,128]{3,2,1,0:T(2,128)(2,1)S(1)}, u32[]{:S(2)}, u32[]{:S(2)}) async-start(bf16[128,49,2,128]{3,2,1,0:T(2,128)(2,1)} %shard_map.74), calls=%async_computation.1 | async-start | bytes 6422528 | tf_op jit(solution)/shard_map/all_to_all | solution.py:347
  67.4 5.8 %copy-start = (bf16[128,49,2,128]{3,2,1,0:T(2,128)(2,1)}, bf16[128,49,2,128]{3,2,1,0:T(2,128)(2,1)S(1)}, u32[]{:S(2)}) copy-start(bf16[128,49,2,128]{3,2,1,0:T(2,128)(2,1)S(1)} %all-to-all-done.1.refs_0_) | copy-start | bytes 9633796
  67.4 46.5 %all-to-all-start = ((bf16[128,96,128]{2,1,0:T(8,128)(2,1)}), bf16[128,96,128]{2,1,0:T(8,128)(2,1)}, u32[]{:S(2)}, u32[]{:S(2)}) async-start(bf16[128,96,128]{2,1,0:T(8,128)(2,1)} %shard_map.73), calls=%async_computation | async-start | bytes 6291456 | tf_op jit(solution)/shard_map/all_to_all | solution.py:348

commit v7 on v5

--- a/solution.py
+++ b/solution.py
@@ -91,6 +91,7 @@
         at = pl.ds(layer * height[0] if noted else pl.multiple_of(layer * SLAB_SLOTS, 16), height[0])
         for tile in range(VALUES // 128):
             pieces = [placed[side, :, tile * 128 : tile * 128 + 128] for side in range(SIDE)]
+            pieces = [pltpu.roll(p, side * SPAN, 1) if side else p for side, p in enumerate(pieces)]
             for k in range(SIDE):
                 joined = pieces[(SIDE - 1 - k) % SIDE]
                 for g in range(SIDE - 1):
@@ -121,7 +122,7 @@
             )
             for tile in range(VALUES // 128):
                 lanes = slice(tile * 128, tile * 128 + 128)
-                placed[side, :, lanes] = pltpu.roll(found[:, lanes], side * SPAN, 1)
+                placed[side, :, lanes] = found[:, lanes]
 
         small = skip + count <= NREC
 
@@ -271,7 +272,7 @@
         layer, part = p // PARTS, lax.rem(p, PARTS)
         wide[:, :PART] = raw[:, part_rows(p)].reshape(DEVICES, PART, 128).astype(jnp.float32)
         for s in range(PART):
-            turned = jnp.transpose(flat[pl.ds(s, DEVICES, stride=WIDE), :])
+            turned = jnp.transpose(flat[pl.ds(s, DEVICES, stride=WIDE), :].astype(jnp.bfloat16)).astype(jnp.float32)
             for side in range(SIDE):
                 for c in range(2):
                     at = side * SPAN + c * FC

time: 121 us -> 122 us (level)
  transfers between devices with their start and end apart: 2 -> 2, of which waited for: 2 -> 2; matrix products, arithmetic and copies ran while one was open for 1% -> 1% of each run, Pallas kernels for 34% -> 33%
where the time goes in v7:
time: 122 us; the launch traced here: 121 us
  Pallas kernels  62.4 us (51%)
  waiting for transfers between devices  40.4 us (33%)
  starting transfers between devices  17.1 us (14%)
    pallas_call x2, Pallas kernels, spread(): pl.pallas_call(spread_kernel, in_specs=[scalars, scalars, scalars, pl.Blo...  28.8 us
    all_to_all x1, waiting for transfers between devices, on_device(): lax.all_to_all(spread(0, traces, *own), everyone, split_axis=0, concat_ax...  28.3 us
    pallas_call x2, Pallas kernels, phases(): pl.pallas_call(phase_kernel, grid=(SHOTS // PHASE_ROWS,), in_specs=[pl.Bl...  19.6 us
    pallas_call x2, Pallas kernels, encode(): pl.pallas_call(kernel, in_specs=[anywhere] * len(operands), out_specs=any...  14 us
    all_to_all x1, waiting for transfers between devices, on_device(): lax.all_to_all(spread(1, traces, *own), everyone, split_axis=0, concat_ax...  12.2 us
    all_to_all x1, starting transfers between devices, on_device(): lax.all_to_all(spread(0, traces, *own), everyone, split_axis=0, concat_ax...  11.4 us
    all_to_all x1, starting transfers between devices, on_device(): lax.all_to_all(spread(1, traces, *own), everyone, split_axis=0, concat_ax...  5.75 us
  transfers between devices with their start and end apart: 2, of which 2 were waited for; matrix products, arithmetic and copies ran while one was open for 1% of the time, Pallas kernels for 33%

profile of v7, /device:TPU:1, one launch (start us, length us, event | category | flops | bytes accessed | tf_op | source)
XLA Modules:
  0.0 121.3 jit_solution(5947605966922539786)
XLA Ops:
  0.0 15.6 %shard_map.74 = bf16[128,49,2,128]{3,2,1,0:T(2,128)(2,1)} custom-call(s32[1,8]{1,0:T(1,128)} %counts.3, s32[8]{0:T(128)} %starts.3, s32[8]{0:T(128)} %positions.3, s32[1,512]{1,0:T(1,128)} %bitcast.10, bf16[3072,2048]{1,0:T(8,128)(2,1)} %traces.3, bf16[2048,256]{1,0:T(8,128)(2,1)} %constant.27.clone.table), custom_call_target="tpu_custom_call" | custom-call | tf_op jit(solution)/shard_map/pallas_call | solution.py:171
  15.6 11.4 %all-to-all-start.1 = ((bf16[128,49,2,128]{3,2,1,0:T(2,128)(2,1)}), bf16[128,49,2,128]{3,2,1,0:T(2,128)(2,1)S(1)}, u32[]{:S(2)}, u32[]{:S(2)}) async-start(bf16[128,49,2,128]{3,2,1,0:T(2,128)(2,1)} %shard_map.74), calls=%async_computation.1 | async-start | bytes 6422528 | tf_op jit(solution)/shard_map/all_to_all | solution.py:348
  27.0 13.3 %shard_map.73 = bf16[128,96,128]{2,1,0:T(8,128)(2,1)} custom-call(s32[1,8]{1,0:T(1,128)} %counts.3, s32[8]{0:T(128)} %starts.3, s32[8]{0:T(128)} %positions.3, s32[1,512]{1,0:T(1,128)} %bitcast.11, bf16[3072,2048]{1,0:T(8,128)(2,1)} %traces.3, bf16[2048,256]{1,0:T(8,128)(2,1)} %constant.28.clone.table), custom_call_target="tpu_custom_call" | custom-call | tf_op jit(solution)/shard_map/pallas_call | solution.py:171
  40.2 28.3 %all-to-all-done.1.refs_0_ = bf16[128,49,2,128]{3,2,1,0:T(2,128)(2,1)S(1)} async-done(((bf16[128,49,2,128]{3,2,1,0:T(2,128)(2,1)}), bf16[128,49,2,128]{3,2,1,0:T(2,128)(2,1)S(1)}, u32[]{:S(2)}, u32[]{:S(2)}) %all-to-all-start.1) | async-done | bytes 3211296 | tf_op jit(solution)/shard_map/all_to_all | solution.py:348
  68.5 0.0 copy-start
  68.5 5.7 %all-to-all-start = ((bf16[128,96,128]{2,1,0:T(8,128)(2,1)}), bf16[128,96,128]{2,1,0:T(8,128)(2,1)}, u32[]{:S(2)}, u32[]{:S(2)}) async-start(bf16[128,96,128]{2,1,0:T(8,128)(2,1)} %shard_map.73), calls=%async_computation | async-start | bytes 6291456 | tf_op jit(solution)/shard_map/all_to_all | solution.py:349
  74.3 0.1 slice_convert_fusion
  74.4 0.0 copy-done
  74.4 0.1 fusion
  74.5 1.0 broadcast_in_dim.8.positions
  75.5 9.8 %shard_map.76.refs_1_ = bf16[16,1024,256]{2,1,0:T(8,128)(2,1)} custom-call(s32[1]{0:T(128)} %bitcast.1.first_bin, s32[1024,128]{1,0:T(8,128)} %broadcast_in_dim.8.positions), custom_call_target="tpu_custom_call" | custom-call | tf_op jit(solution)/shard_map/pallas_call | solution.py:221
  85.3 9.8 %shard_map.75.refs_1_ = bf16[16,1024,256]{2,1,0:T(8,128)(2,1)} custom-call(s32[1]{0:T(128)S(6)} %add.13.first_bin, s32[1024,128]{1,0:T(8,128)} %broadcast_in_dim.8.positions), custom_call_target="tpu_custom_call" | custom-call | tf_op jit(solution)/shard_map/pallas_call | solution.py:221
  95.1 7.7 %shard_map.77.refs_2_ = bf16[48,16,256]{2,1,0:T(8,128)(2,1)} custom-call(bf16[128,49,2,128]{3,2,1,0:T(2,128)(2,1)} %copy-done, bf16[16,1024,256]{2,1,0:T(8,128)(2,1)} %shard_map.76.refs_1_), custom_call_target="tpu_custom_call" | custom-call | tf_op jit(solution)/shard_map/pallas_call | solution.py:325
  102.8 12.2 %all-to-all-done.refs_0_ = bf16[128,96,128]{2,1,0:T(8,128)(2,1)} async-done(((bf16[128,96,128]{2,1,0:T(8,128)(2,1)}), bf16[128,96,128]{2,1,0:T(8,128)(2,1)}, u32[]{:S(2)}, u32[]{:S(2)}) %all-to-all-start) | async-done | bytes 3145760 | tf_op jit(solution)/shard_map/all_to_all | solution.py:349
  115.0 6.3 %shard_map.78 = bf16[48,32,256]{2,1,0:T(8,128)(2,1)} custom-call(bf16[128,96,128]{2,1,0:T(8,128)(2,1)} %all-to-all-done.refs_0_, bf16[16,1024,256]{2,1,0:T(8,128)(2,1)} %shard_map.75.refs_1_, bf16[48,16,256]{2,1,0:T(8,128)(2,1)} %shard_map.77.refs_2_), custom_call_target="tpu_custom_call" | custom-call | tf_op jit(solution)/shard_map/pallas_call | solution.py:325
  (2 shorter events, 0.1 us)
Async XLA Ops:
  15.6 53.0 %all-to-all-start.1 = ((bf16[128,49,2,128]{3,2,1,0:T(2,128)(2,1)}), bf16[128,49,2,128]{3,2,1,0:T(2,128)(2,1)S(1)}, u32[]{:S(2)}, u32[]{:S(2)}) async-start(bf16[128,49,2,128]{3,2,1,0:T(2,128)(2,1)} %shard_map.74), calls=%async_computation.1 | async-start | bytes 6422528 | tf_op jit(solution)/shard_map/all_to_all | solution.py:348
  68.5 5.8 %copy-start = (bf16[128,49,2,128]{3,2,1,0:T(2,128)(2,1)}, bf16[128,49,2,128]{3,2,1,0:T(2,128)(2,1)S(1)}, u32[]{:S(2)}) copy-start(bf16[128,49,2,128]{3,2,1,0:T(2,128)(2,1)S(1)} %all-to-all-done.1.refs_0_) | copy-start | bytes 9633796
  68.5 46.5 %all-to-all-start = ((bf16[128,96,128]{2,1,0:T(8,128)(2,1)}), bf16[128,96,128]{2,1,0:T(8,128)(2,1)}, u32[]{:S(2)}, u32[]{:S(2)}) async-start(bf16[128,96,128]{2,1,0:T(8,128)(2,1)} %shard_map.73), calls=%async_computation | async-start | bytes 6291456 | tf_op jit(solution)/shard_map/all_to_all | solution.py:349
